TPU v7x, 32 devices: a whole 2x2x4 slice. The times are simulated.
32 devices in a mesh: dp: 2 (over core), lat: 4 (over z), lon: 4 (over y, x).
Axes of the slice: x: 2, y: 2, z: 4, core: 2. Of those that a mesh axis runs over, the one named last changes fastest.
Arguments:
- fields: bfloat16 [2, 320, 512, 128], P('dp', 'lat', 'lon'), may hold values from -6 to 6
- down_weight: bfloat16 [3, 3, 128, 128], P(None, None, 'dp'), may hold values from -0.1875 to 0.1875
- mid_weight: bfloat16 [3, 3, 128, 128], P(None, None, 'dp'), may hold values from -0.1875 to 0.1875
- up_weight: bfloat16 [3, 3, 128, 128], P(None, None, 'dp'), may hold values from -0.1875 to 0.1875
- cotangent: bfloat16 [2, 320, 512, 128], P('dp', 'lat', 'lon'), may hold values from -6 to 6
Outputs:
- level_out: bfloat16 [2, 320, 512, 128], P('dp', 'lat', 'lon')
- grad_fields: bfloat16 [2, 320, 512, 128], P('dp', 'lat', 'lon')
- grad_down: float32 [3, 3, 128, 128], P(None, None, 'dp')
- grad_mid: float32 [3, 3, 128, 128], P(None, None, 'dp')
- grad_up: float32 [3, 3, 128, 128], P(None, None, 'dp')
All inputs are finite; a program needn't handle non-finite values.
Results may differ from a plain program's by a relative error of at most 0.012.
Values may be sent and summed in bfloat16 or wider, within the bound.
A program may use at most 128 MiB of HBM per device.

v0:
```python
import functools
import math

import jax
import jax.numpy as jnp
from jax import lax
from jax.experimental import pallas as pl
from jax.experimental.pallas import tpu as pltpu
from jax.sharding import PartitionSpec as P

EDGE = 8
BF = jnp.bfloat16
F32 = jnp.float32


def dot(a, b):
    return lax.dot_general(a, b, (((1,), (0,)), ((), ())), preferred_element_type=F32)


def dot_t(a, b):
    return lax.dot_general(a, b, (((0,), (0,)), ((), ())), preferred_element_type=F32)


def rolled(x, by):
    return pltpu.roll(x, by % x.shape[0], 0)


def lanes(*parts):
    return jnp.concatenate(parts, axis=-1)


def blocks(rows):
    return jnp.concatenate([lanes(*row) for row in rows], axis=0)


def strided_block(w, r, z):
    return blocks([[w(r, 1), z], [w(r, 2), w(r, 0)]])


def spread_block(w, r, z):
    return blocks([[w(r, 1), w(r, 2)], [z, w(r, 0)]])


def paired_block(w, c, z):
    return blocks([[w(0, c), z], [w(1, c), w(0, c)], [w(2, c), w(1, c)], [z, w(2, c)]])


def flat(x):
    return x.reshape(x.shape[0] * x.shape[1], x.shape[2])


def compute(half, scale, f, c, wd, wm, wu, out, gout, grads,
            bd, bg, bm, bn, bu, bf, dp, gps, gpp, s1, s2, acc_u, acc_m, acc_d):
    wide = f.shape[2]
    ch = f.shape[3] // 2
    cols = wide - 2 * EDGE
    z = jnp.zeros((ch, ch), BF)
    lat = lax.axis_index("lat")
    first = lat == 0
    last = lat == lax.axis_size("lat") - 1
    low = jnp.where(first, 0, -(1 << 20))
    high = jnp.where(last, half, 1 << 20)

    def plain(ref):
        return lambda r, k: ref[r, k]

    def turned(ref):
        return lambda r, k: ref[r, k].T

    def flipped(ref):
        return lambda r, k: ref[2 - r, 2 - k].T

    for r in range(3):
        at = pl.ds(2 * ch * r, 2 * ch)
        bd[at, :] = strided_block(plain(wd), r, z)
        bg[at, :] = strided_block(turned(wu), r, z)
        bu[at, :] = spread_block(plain(wu), r, z)
        bf[at, :] = spread_block(turned(wd), r, z)
        bm[:, at] = paired_block(plain(wm), r, z)
        bn[:, at] = paired_block(flipped(wm), r, z)

    def inside(rows):
        return jnp.logical_and(rows >= low, rows < high)

    def row_mask(n, base, shape_cols):
        rows = base + lax.broadcasted_iota(jnp.int32, (n, wide, shape_cols), 0)
        return inside(rows)

    def pair_mask(n, base):
        shape = (n, wide, 2 * ch)
        rows = (base + 2 * lax.broadcasted_iota(jnp.int32, shape, 0)
                + (lax.broadcasted_iota(jnp.int32, shape, 2) >= ch).astype(jnp.int32))
        return inside(rows)

    def strided(src, start, n, weight):
        x0 = src[pl.ds(start, n), 1]
        x1 = src[pl.ds(start + 1, n), 0]
        x2 = src[pl.ds(start + 1, n), 1]
        acc = dot(flat(lanes(x0, x1, x2)), weight[...])
        return acc[:, :ch] + rolled(acc[:, ch:], 1)

    def to_pairs(x, n):
        x = x.reshape(n, 2, wide, ch)
        return lanes(x[:, 0], x[:, 1])

    def same(src, start, n, weight):
        acc = dot(flat(lanes(src[pl.ds(start, n)], src[pl.ds(start + 1, n)])), weight[...])
        k = 2 * ch
        total = rolled(acc[:, :k], 1) + acc[:, k:2 * k] + rolled(acc[:, 2 * k:], -1)
        return total

    pairs = (half + 8) // 2
    nd = 6 if pairs % 6 == 0 else 1

    def down_step(t, _):
        q = t * nd
        v = strided(f, 2 * q, 2 * nd, bd)
        v = to_pairs(v, nd)
        dp[pl.ds(q, nd)] = jnp.where(pair_mask(nd, 2 * q - 3), v, 0.0).astype(BF)
        return 0

    lax.fori_loop(0, pairs // nd, down_step, 0)

    def shifted_rows(dst, start, n, v):
        nxt = rolled(v, -1)
        for a in range(2):
            half_lanes = slice(a * ch, (a + 1) * ch)
            piece = lanes(v[:, half_lanes], nxt[:, half_lanes]).astype(BF)
            dst[pl.ds(start, n), a] = piece.reshape(n, wide, 2 * ch)

    pairs_mid = (half + 4) // 2
    nm = 11 if pairs_mid % 11 == 0 else 1

    def mid_step(t, _):
        p = t * nm
        pre = same(dp, p, nm, bm)
        g = strided(c, 2 * p + 1, 2 * nm, bg)
        g = flat(to_pairs(g, nm))
        sig = jax.nn.sigmoid(pre)
        ok = flat(pair_mask(nm, 2 * p - 2))
        mid = jnp.where(ok, pre * sig, 0.0)
        gp = jnp.where(ok, g * sig * (1.0 + pre * (1.0 - sig)), 0.0)
        shifted_rows(s1, p, nm, mid)
        gpp[pl.ds(p, nm)] = gp.astype(BF).reshape(nm, wide, 2 * ch)
        place = lax.broadcasted_iota(jnp.int32, (nm, wide, 2 * ch), 1)
        own = flat(jnp.logical_and(place >= EDGE, place < EDGE + cols))
        gm = jnp.where(own, gp, 0.0)
        after, before = rolled(gm, -1), rolled(gm, 1)
        for a in range(2):
            k = slice(a * ch, (a + 1) * ch)
            piece = lanes(after[:, k], gm[:, k], before[:, k]).astype(BF)
            gps[pl.ds(p, nm), a] = piece.reshape(nm, wide, 3 * ch)
        return 0

    lax.fori_loop(0, pairs_mid // nm, mid_step, 0)

    pairs_gd = (half + 2) // 2
    ng = 7 if pairs_gd % 7 == 0 else 1

    def gd_step(t, _):
        q = t * ng
        v = same(gpp, q, ng, bn)
        v = jnp.where(flat(pair_mask(ng, 2 * q - 1)), v, 0.0)
        shifted_rows(s2, q, ng, v)
        return 0

    lax.fori_loop(0, pairs_gd // ng, gd_step, 0)

    acc_u[...] = jnp.zeros_like(acc_u)
    acc_m[...] = jnp.zeros_like(acc_m)
    acc_d[...] = jnp.zeros_like(acc_d)
    place = lax.broadcasted_iota(jnp.int32, (wide, 2 * ch), 0)
    place = place + (lax.broadcasted_iota(jnp.int32, (wide, 2 * ch), 1) >= ch).astype(jnp.int32)
    own = jnp.logical_and(place >= EDGE, place < EDGE + cols).astype(F32).astype(BF)[None]
    step = 4

    def taps(src, i, n):
        return flat(lanes(src[pl.ds(i + 3, n), 1], src[pl.ds(i + 4, n), 0], src[pl.ds(i + 4, n), 1]))

    def grads_step(t, _):
        p = t * step
        n = 2 * step
        i = 2 * p
        m = s1[pl.ds(p + 1, step)].reshape(n, wide, 2 * ch) * own
        acc_u[...] += dot_t(flat(m), taps(c, i, n))
        ga = s2[pl.ds(p, step + 1)].reshape(2 * step + 2, wide, 2 * ch)[1:1 + n] * own
        acc_d[...] += dot_t(flat(ga), taps(f, i, n))
        d0, d1 = dp[pl.ds(p + 1, step)], dp[pl.ds(p + 2, step)]
        acc_m[...] += (
            dot_t(flat(gps[pl.ds(p + 1, step), 0]), flat(lanes(d0, d1[:, :, :ch])))
            + dot_t(flat(gps[pl.ds(p + 1, step), 1]), flat(lanes(d0[:, :, ch:], d1)))
        )
        return 0

    lax.fori_loop(0, half // (2 * step), grads_step, 0)

    for r in range(3):
        for k in range(3):
            top = ch if k == 0 else 0
            left = 2 * ch * r + (0 if k == 1 else ch)
            tap = 3 * r + k
            grads[tap] = (acc_d[top:top + ch, left:left + ch] * scale).T.astype(BF)
            grads[9 + tap] = (acc_m[k * ch:(k + 1) * ch, r * ch:(r + 1) * ch] * scale).T.astype(BF)
            grads[18 + tap] = (acc_u[top:top + ch, left:left + ch] * scale).astype(BF)

    def up_step(t, _):
        i = t * n_up
        def rows1(at, n):
            q = t * (n_up // 2) + 1
            return s1[pl.ds(q, n // 2 + 1)].reshape(n + 2, wide, 2 * ch)[at:at + n]
        def rows2(at, n):
            q = t * (n_up // 2)
            return s2[pl.ds(q, n // 2 + 1)].reshape(n + 2, wide, 2 * ch)[at + 1:at + 1 + n]
        for rows, base, dst, weight in ((rows1, f, out, bu), (rows2, c, gout, bf)):
            lo, hi = flat(rows(0, n_up)), flat(rows(1, n_up))
            k = 2 * ch
            even = dot(lo, weight[k:2 * k, :])
            odd = dot(lo, weight[2 * k:, :]) + dot(hi, weight[:k, :])
            for a, v in enumerate((even, odd)):
                v = v.reshape(n_up, wide, k) + base[pl.ds(i + 4, n_up), a].astype(F32)
                dst[pl.ds(i, n_up), a] = v[:, EDGE:EDGE + cols].astype(BF)
        return 0

    n_up = 8
    lax.fori_loop(0, half // n_up, up_step, 0)


def shifted(x, axis, width, dim, periodic):
    count = lax.axis_size(axis)
    forward = [(i, i + 1) for i in range(count - 1)]
    if periodic:
        forward.append((count - 1, 0))
    backward = [(b, a) for a, b in forward]
    low = lax.ppermute(lax.slice_in_dim(x, x.shape[dim] - width, None, axis=dim), axis, forward)
    high = lax.ppermute(lax.slice_in_dim(x, 0, width, axis=dim), axis, backward)
    return low, high


def body(fields, down_weight, mid_weight, up_weight, cotangent):
    _, rows, full, ch = fields.shape
    half, cols = rows // 2, full // 2
    wide = cols + 2 * EDGE
    weights = jnp.stack([down_weight, mid_weight, up_weight])
    weights = lax.all_gather(weights, "dp", axis=3, tiled=True)
    cells = (lax.axis_size("dp") * rows * lax.axis_size("lat") * full * lax.axis_size("lon"))
    scale = 1.0 / math.sqrt(cells)
    x = jnp.stack([fields[0], cotangent[0]]).reshape(2, rows, cols, 2 * ch)
    low, high = shifted(x, "lat", 8, 1, False)
    tall = jnp.concatenate([low, x, high, jnp.zeros((2, 2, cols, 2 * ch), BF)], axis=1)
    low, high = shifted(tall, "lon", 4, 2, True)
    gap = jnp.zeros((2, rows + 18, EDGE - 4, 2 * ch), BF)
    whole = jnp.concatenate([gap, low, tall, high, gap], axis=2)
    whole = whole.reshape(2, half + 9, 2, wide, 2 * ch)
    k = 2 * ch
    vm = pl.BlockSpec(memory_space=pltpu.VMEM)
    out, gout, grads = pl.pallas_call(
        functools.partial(compute, half, scale),
        out_shape=(
            jax.ShapeDtypeStruct((half, 2, cols, k), BF),
            jax.ShapeDtypeStruct((half, 2, cols, k), BF),
            jax.ShapeDtypeStruct((27, ch, ch), BF),
        ),
        in_specs=[vm] * 5,
        out_specs=(vm, vm, vm),
        scratch_shapes=[
            pltpu.VMEM((3 * k, k), BF),
            pltpu.VMEM((3 * k, k), BF),
            pltpu.VMEM((2 * k, 3 * k), BF),
            pltpu.VMEM((2 * k, 3 * k), BF),
            pltpu.VMEM((3 * k, k), BF),
            pltpu.VMEM((3 * k, k), BF),
            pltpu.VMEM(((half + 8) // 2, wide, k), BF),
            pltpu.VMEM(((half + 4) // 2, 2, wide, 3 * ch), BF),
            pltpu.VMEM(((half + 4) // 2, wide, k), BF),
            pltpu.VMEM(((half + 4) // 2, 2, wide, k), BF),
            pltpu.VMEM(((half + 2) // 2, 2, wide, k), BF),
            pltpu.VMEM((k, 3 * k), F32),
            pltpu.VMEM((3 * ch, 3 * ch), F32),
            pltpu.VMEM((k, 3 * k), F32),
        ],
        compiler_params=pltpu.CompilerParams(vmem_limit_bytes=50 << 20),
    )(whole[0], whole[1], weights[0], weights[1], weights[2])
    mine = lax.psum_scatter(grads, "dp", scatter_dimension=1, tiled=True)
    total = lax.psum(mine.astype(F32), ("lat", "lon"))
    total = total.reshape(3, 3, 3, ch // lax.axis_size("dp"), ch)
    return (
        out.reshape(1, rows, full, ch),
        gout.reshape(1, rows, full, ch),
        total[0],
        total[1],
        total[2],
    )


def solution(mesh):
    maps = P("dp", "lat", "lon", None)
    kernel = P(None, None, "dp", None)
    return jax.shard_map(
        body,
        mesh=mesh,
        in_specs=(maps, kernel, kernel, kernel, maps),
        out_specs=(maps, maps, kernel, kernel, kernel),
        check_vma=False,
    )
```

profile of v0, /device:TPU:0, one launch (start us, length us, event | category | flops | bytes accessed | tf_op | source)
XLA Modules:
  0.0 234.9 jit_solution(322069331625713578)
XLA Ops:
  7.2 5.3 %pad_maximum_fusion = bf16[2,80,128,128]{3,2,1,0:T(8,128)(2,1)} fusion(bf16[1,80,128,128]{3,2,1,0:T(8,128)(2,1)} %param.9, bf16[1,80,128,128]{3,2,1,0:T(8,128)(2,1)} %param.5), kind=kLoop, calls=%fused_computation.1 | loop fusion | flops 2621440 | bytes 10485760 | tf_op jit(solution)/shard_map/stack | solution.py:247
  12.5 8.6 %reshape.31 = bf16[2,80,64,256]{3,2,1,0:T(8,128)(2,1)} reshape(bf16[2,80,128,128]{3,2,1,0:T(8,128)(2,1)} %pad_maximum_fusion) | data formatting | bytes 10485760 | tf_op jit(solution)/shard_map/reshape | solution.py:247
  21.1 1.3 fusion.2
  22.4 5.0 %collective-permute-start = (bf16[2,8,64,256]{3,2,1,0:T(8,128)(2,1)S(1)}, bf16[2,8,64,256]{3,2,1,0:T(8,128)(2,1)S(1)}, u32[]{:S(2)}, u32[]{:S(2)}) collective-permute-start(bf16[2,8,64,256]{3,2,1,0:T(8,128)(2,1)S(1)} %get-tuple-element.15), channel_id=1, source_target_pairs={{0,4},{4,8},{8,12},{1,5},{5,9},{9,13},{2,6},{6,10},{10,14},{3,7},{... | collective-permute-start | bytes 1572872 | tf_op jit(solution)/shard_map/ppermute | solution.py:234
  27.4 1.3 collective-permute-start.1
  28.7 0.1 pad.6.clone
  28.8 9.7 %collective-permute-done = bf16[2,8,64,256]{3,2,1,0:T(8,128)(2,1)S(1)} collective-permute-done((bf16[2,8,64,256]{3,2,1,0:T(8,128)(2,1)S(1)}, bf16[2,8,64,256]{3,2,1,0:T(8,128)(2,1)S(1)}, u32[]{:S(2)}, u32[]{:S(2)}) %collective-permute-start) | collective-permute-done | bytes 524320 | tf_op jit(solution)/shard_map/ppermute | solution.py:234
  38.5 4.1 %collective-permute-done.1 = bf16[2,8,64,256]{3,2,1,0:T(8,128)(2,1)S(1)} collective-permute-done((bf16[2,8,64,256]{3,2,1,0:T(8,128)(2,1)S(1)}, bf16[2,8,64,256]{3,2,1,0:T(8,128)(2,1)S(1)}, u32[]{:S(2)}, u32[]{:S(2)}) %collective-permute-start.1) | collective-permute-done | bytes 524320 | tf_op jit(solution)/shard_map/ppermute | solution.py:235
  42.7 4.7 %maximum_maximum_fusion = bf16[2,98,64,256]{3,2,1,0:T(8,128)(2,1)S(1)} fusion(bf16[2,8,64,256]{3,2,1,0:T(8,128)(2,1)S(1)} %collective-permute-done.1, bf16[2,80,64,256]{3,2,1,0:T(8,128)(2,1)} %reshape.31, bf16[2,8,64,256]{3,2,1,0:T(8,128)(2,1)S(1)} %collective-permute-done, bf16[98]{0:T(256)(128)(2,1)S(1)} %pad.6.clone), kind=kLoop, calls=%fused_computation | loop fusion | flops 9633792 | bytes 12714180 | tf_op jit(solution)/shard_map/concatenate | solution.py:249
  47.4 0.3 fusion.1
  47.7 1.5 collective-permute-start.2
  49.3 1.4 collective-permute-start.3
  50.7 2.4 %all_gather.3 = bf16[3,3,3,128,128]{4,3,2,1,0:T(8,128)(2,1)S(1)} all-gather(bf16[3,3,3,64,128]{4,3,2,1,0:T(8,128)(2,1)S(1)} %pad_maximum_fusion.1), channel_id=1, replica_groups=mesh['dp'=2,'lat'=4,'lon'=4] {'dp'}, dimensions={3}, use_global_device_ids=true | all-gather | bytes 1327104 | tf_op jit(solution)/shard_map/all_gather | solution.py:244
  53.1 0.1 slice_bitcast_fusion
  53.2 7.7 %collective-permute-done.2 = bf16[2,98,4,256]{3,2,1,0:T(4,128)(2,1)S(1)} collective-permute-done((bf16[2,98,4,256]{3,2,1,0:T(4,128)(2,1)S(1)}, bf16[2,98,4,256]{3,2,1,0:T(4,128)(2,1)S(1)}, u32[]{:S(2)}, u32[]{:S(2)}) %collective-permute-start.2) | collective-permute-done | bytes 401440 | tf_op jit(solution)/shard_map/ppermute | solution.py:234
  60.9 6.3 %collective-permute-done.3 = bf16[2,98,4,256]{3,2,1,0:T(4,128)(2,1)S(1)} collective-permute-done((bf16[2,98,4,256]{3,2,1,0:T(4,128)(2,1)S(1)}, bf16[2,98,4,256]{3,2,1,0:T(4,128)(2,1)S(1)}, u32[]{:S(2)}, u32[]{:S(2)}) %collective-permute-start.3) | collective-permute-done | bytes 401440 | tf_op jit(solution)/shard_map/ppermute | solution.py:235
  67.2 0.1 broadcast_in_dim.6
  67.3 33.7 %concatenate.7 = bf16[2,98,80,256]{3,2,1,0:T(8,128)(2,1)} concatenate(bf16[2,98,4,256]{3,2,1,0:T(4,128)(2,1)S(1)} %broadcast_in_dim.6, bf16[2,98,4,256]{3,2,1,0:T(4,128)(2,1)S(1)} %collective-permute-done.2, bf16[2,98,64,256]{3,2,1,0:T(8,128)(2,1)} %copy-done, bf16[2,98,4,256]{3,2,1,0:T(4,128)(2,1)S(1)} %collective-permute-done.3, bf16[2,98,4,256]{3,2,1,0:T(4,128)(2,1)S(1)} %broadcast_in_dim.6), dimensions={2} | concatenate | bytes 16056320 | tf_op jit(solution)/shard_map/concatenate | solution.py:252
  101.0 5.5 %fusion = (bf16[1,98,80,256]{3,2,1,0:T(8,128)(2,1)}, bf16[1,98,80,256]{3,2,1,0:T(8,128)(2,1)}) fusion(bf16[2,98,80,256]{3,2,1,0:T(8,128)(2,1)} %concatenate.7), kind=kLoop, calls=%fused_computation.6 | loop fusion | bytes 16056320 | tf_op jit(solution)/shard_map/slice | solution.py:282
  106.5 23.9 %shard_map.92 = (bf16[40,2,64,256]{3,2,1,0:T(8,128)(2,1)}, bf16[40,2,64,256]{3,2,1,0:T(8,128)(2,1)}, bf16[27,128,128]{2,1,0:T(8,128)(2,1)}) custom-call(bf16[49,2,80,256]{3,2,1,0:T(8,128)(2,1)} %bitcast.21, bf16[49,2,80,256]{3,2,1,0:T(8,128)(2,1)} %bitcast.20, bf16[3,3,128,128]{3,2,1,0:T(8,128)(2,1)S(1)} %get-tuple-element.22.wd, ...), custom_call_target="tpu_custom_call" | custom-call | tf_op jit(solution)/shard_map/pallas_call | solution.py:256
  130.4 5.2 %reshape.32 = bf16[1,80,128,128]{3,2,1,0:T(8,128)(2,1)} reshape(bf16[40,2,64,256]{3,2,1,0:T(8,128)(2,1)} %get-tuple-element.8) | data formatting | bytes 5242880 | tf_op jit(solution)/shard_map/reshape | solution.py:287
  135.6 2.9 %reshape.33 = bf16[1,80,128,128]{3,2,1,0:T(8,128)(2,1)} reshape(bf16[40,2,64,256]{3,2,1,0:T(8,128)(2,1)S(1)} %copy-done.1) | data formatting | bytes 5242880 | tf_op jit(solution)/shard_map/reshape | solution.py:288
  138.5 88.6 %all-reduce.1 = f32[27,64,128]{2,1,0:T(8,128)S(1)} all-reduce(bf16[27,64,128]{2,1,0:T(8,128)(2,1)} %reduce-scatter.2.cloned.1.call-done), channel_id=1, replica_groups=mesh['dp'=2,'lat'=4,'lon'=4] {'lat','lon'}, use_global_device_ids=true, to_apply=%region_1.0 | all-reduce | flops 221184 | bytes 1327104 | tf_op jit(solution)/shard_map/psum | solution.py:284
  227.1 0.9 fusion.3
  (15 shorter events, 0.1 us)
Async XLA Ops:
  7.2 131.3 %reduce-scatter.2.cloned.1.call-start = ((), (), s32[]{:S(2)}) async-start(), calls=%async_computation.1 | async-start | bytes 1327104 | tf_op jit(solution)/shard_map/reduce_scatter | solution.py:283
  12.5 16.2 %copy-start.2 = (bf16[3,3,64,128]{3,2,1,0:T(8,128)(2,1)S(1)}, bf16[3,3,64,128]{3,2,1,0:T(8,128)(2,1)}, u32[]{:S(2)}) copy-start(bf16[3,3,64,128]{3,2,1,0:T(8,128)(2,1)} %param.8) | copy-start | bytes 442372
  12.5 16.2 %copy-start.3 = (bf16[3,3,64,128]{3,2,1,0:T(8,128)(2,1)S(1)}, bf16[3,3,64,128]{3,2,1,0:T(8,128)(2,1)}, u32[]{:S(2)}) copy-start(bf16[3,3,64,128]{3,2,1,0:T(8,128)(2,1)} %param.7) | copy-start | bytes 442372
  12.5 16.2 %copy-start.4 = (bf16[3,3,64,128]{3,2,1,0:T(8,128)(2,1)S(1)}, bf16[3,3,64,128]{3,2,1,0:T(8,128)(2,1)}, u32[]{:S(2)}) copy-start(bf16[3,3,64,128]{3,2,1,0:T(8,128)(2,1)} %param.6) | copy-start | bytes 442372
  22.4 16.1 %collective-permute-start = (bf16[2,8,64,256]{3,2,1,0:T(8,128)(2,1)S(1)}, bf16[2,8,64,256]{3,2,1,0:T(8,128)(2,1)S(1)}, u32[]{:S(2)}, u32[]{:S(2)}) collective-permute-start(bf16[2,8,64,256]{3,2,1,0:T(8,128)(2,1)S(1)} %get-tuple-element.15), channel_id=1, source_target_pairs={{0,4},{4,8},{8,12},{1,5},{5,9},{9,13},{2,6},{6,10},{10,14},{3,7},{... | collective-permute-start | bytes 1572872 | tf_op jit(solution)/shard_map/ppermute | solution.py:234
  27.4 15.3 %collective-permute-start.1 = (bf16[2,8,64,256]{3,2,1,0:T(8,128)(2,1)S(1)}, bf16[2,8,64,256]{3,2,1,0:T(8,128)(2,1)S(1)}, u32[]{:S(2)}, u32[]{:S(2)}) collective-permute-start(bf16[2,8,64,256]{3,2,1,0:T(8,128)(2,1)S(1)} %get-tuple-element.16), channel_id=1, source_target_pairs={{4,0},{8,4},{12,8},{5,1},{9,5},{13,9},{6,2},{10,6},{14,10},{7,3},{... | collective-permute-start | bytes 1572872 | tf_op jit(solution)/shard_map/ppermute | solution.py:235
  47.4 3.3 %copy-start = (bf16[2,98,64,256]{3,2,1,0:T(8,128)(2,1)}, bf16[2,98,64,256]{3,2,1,0:T(8,128)(2,1)S(1)}, u32[]{:S(2)}) copy-start(bf16[2,98,64,256]{3,2,1,0:T(8,128)(2,1)S(1)} %maximum_maximum_fusion) | copy-start | bytes 19267588
  47.7 13.2 %collective-permute-start.2 = (bf16[2,98,4,256]{3,2,1,0:T(4,128)(2,1)S(1)}, bf16[2,98,4,256]{3,2,1,0:T(4,128)(2,1)S(1)}, u32[]{:S(2)}, u32[]{:S(2)}) collective-permute-start(bf16[2,98,4,256]{3,2,1,0:T(4,128)(2,1)S(1)} %get-tuple-element.14), channel_id=1, source_target_pairs={{0,1},{1,2},{2,3},{3,0},{4,5},{5,6},{6,7},{7,4},{8,9},{9,10},{10,1... | collective-permute-start | bytes 1204232 | tf_op jit(solution)/shard_map/ppermute | solution.py:234
  49.3 17.9 %collective-permute-start.3 = (bf16[2,98,4,256]{3,2,1,0:T(4,128)(2,1)S(1)}, bf16[2,98,4,256]{3,2,1,0:T(4,128)(2,1)S(1)}, u32[]{:S(2)}, u32[]{:S(2)}) collective-permute-start(bf16[2,98,4,256]{3,2,1,0:T(4,128)(2,1)S(1)} %get-tuple-element.13), channel_id=1, source_target_pairs={{1,0},{2,1},{3,2},{0,3},{5,4},{6,5},{7,6},{4,7},{9,8},{10,9},{11,1... | collective-permute-start | bytes 1204232 | tf_op jit(solution)/shard_map/ppermute | solution.py:235
  130.4 5.2 %copy-start.1 = (bf16[40,2,64,256]{3,2,1,0:T(8,128)(2,1)S(1)}, bf16[40,2,64,256]{3,2,1,0:T(8,128)(2,1)}, u32[]{:S(2)}) copy-start(bf16[40,2,64,256]{3,2,1,0:T(8,128)(2,1)} %get-tuple-element.9) | copy-start | bytes 7864324
Sparse Core Ops, SparseCore 0:
  130.5 7.5 reduce-scatter.1
where the time goes:
time: 236 us; the launch traced here: 235 us
  blocking collectives  91 us (39%)
  local copies, waits for them, and re-layouts  58.7 us (25%)
  waiting for transfers between devices  27.8 us (12%)
  Pallas kernels  23.9 us (10%)
  between operations  14.1 us (6%)
  other arithmetic  10.1 us (4%)
  starting transfers between devices  9.27 us (4%)
    psum x1, blocking collectives, body(): total = lax.psum(mine.astype(F32), ('lat', 'lon'))  88.6 us
    concatenate x1, local copies, waits for them, and re-layouts, body(): whole = jnp.concatenate([gap, low, tall, high, gap], axis=2)  33.7 us
    pallas_call x1, Pallas kernels, body(): pl.pallas_call(functools.partial(compute, half, scale), out_shape=(jax.Sh...  23.9 us
    ppermute x2, waiting for transfers between devices, shifted(): lax.ppermute(lax.slice_in_dim(x, x.shape[dim] - width, None, axis=dim), a...  17.4 us
    ppermute x2, waiting for transfers between devices, shifted(): high = lax.ppermute(lax.slice_in_dim(x, 0, width, axis=dim), axis, backward)  10.4 us
    reshape x1, local copies, waits for them, and re-layouts, body(): x = jnp.stack([fields[0], cotangent[0]]).reshape(2, rows, cols, 2 * ch)  8.61 us
    ppermute x2, starting transfers between devices, shifted(): lax.ppermute(lax.slice_in_dim(x, x.shape[dim] - width, None, axis=dim), a...  6.5 us
    slice x1, local copies, waits for them, and re-layouts, body(): whole[1]  5.53 us
  transfers between devices with their start and end apart: 5, of which 4 were waited for; matrix products, arithmetic and copies ran while one was open for 4% of the time, Pallas kernels for 0%

commit v1 on v0

--- a/solution.py
+++ b/solution.py
@@ -9,6 +9,7 @@
 from jax.sharding import PartitionSpec as P
 
 EDGE = 8
+HALO = 8
 BF = jnp.bfloat16
 F32 = jnp.float32
 
@@ -49,8 +50,10 @@
     return x.reshape(x.shape[0] * x.shape[1], x.shape[2])
 
 
-def compute(half, scale, f, c, wd, wm, wu, out, gout, grads,
-            bd, bg, bm, bn, bu, bf, dp, gps, gpp, s1, s2, acc_u, acc_m, acc_d):
+def compute(scale, raw_f, raw_c, rows_in, cols_in, corners, w_in, out, gout, grads,
+            f, c, tmp, otmp, bd, bg, bm, bn, bu, bf, dp, gps, gpp, s1, s2, acc_u, acc_m, acc_d):
+    half = raw_f.shape[0] // 2
+    wd, wm, wu = w_in.at[0], w_in.at[1], w_in.at[2]
     wide = f.shape[2]
     ch = f.shape[3] // 2
     cols = wide - 2 * EDGE
@@ -108,6 +111,31 @@
         k = 2 * ch
         total = rolled(acc[:, :k], 1) + acc[:, k:2 * k] + rolled(acc[:, 2 * k:], -1)
         return total
+
+    side = jnp.zeros((8, HALO, ch), F32)
+    full = 2 * cols
+    tmp[:, 0:HALO, :] = side
+    tmp[:, full + 3 * HALO:, :] = side
+
+    def lay(dst, pair, middle, lower, upper):
+        tmp[:, HALO:2 * HALO, :] = lower.astype(F32).reshape(8, HALO, ch)
+        tmp[:, 2 * HALO:2 * HALO + full, :] = middle.astype(F32)
+        tmp[:, 2 * HALO + full:3 * HALO + full, :] = upper.astype(F32).reshape(8, HALO, ch)
+        even = tmp[:, pl.ds(0, wide, stride=2), :]
+        odd = tmp[:, pl.ds(1, wide, stride=2), :]
+        dst[pl.ds(pair, 4)] = lanes(even, odd).astype(BF).reshape(4, 2, wide, 2 * ch)
+
+    for a, (dst, raw) in enumerate(((f, raw_f), (c, raw_c))):
+        lay(dst, 0, rows_in[a, 0], corners[0, 0, a], corners[0, 1, a])
+        lay(dst, half + 4, rows_in[a, 1], corners[1, 0, a], corners[1, 1, a])
+        dst[half + 8] = jnp.zeros((2, wide, 2 * ch), BF)
+
+        def lay_step(t, _, a=a, dst=dst, raw=raw):
+            lay(dst, 4 * t + 4, raw[pl.ds(8 * t, 8)], cols_in[0, a, pl.ds(4 * t, 4)],
+                cols_in[1, a, pl.ds(4 * t, 4)])
+            return 0
+
+        lax.fori_loop(0, half // 4, lay_step, 0)
 
     pairs = (half + 8) // 2
     nd = 6 if pairs % 6 == 0 else 1
@@ -194,14 +222,24 @@
 
     lax.fori_loop(0, half // (2 * step), grads_step, 0)
 
+    part = ch // 2
+
+    def put(tap, value):
+        value = value.astype(BF)
+        for h in range(2):
+            grads[h, tap * part:(tap + 1) * part, :] = value[h * part:(h + 1) * part]
+
     for r in range(3):
         for k in range(3):
             top = ch if k == 0 else 0
             left = 2 * ch * r + (0 if k == 1 else ch)
             tap = 3 * r + k
-            grads[tap] = (acc_d[top:top + ch, left:left + ch] * scale).T.astype(BF)
-            grads[9 + tap] = (acc_m[k * ch:(k + 1) * ch, r * ch:(r + 1) * ch] * scale).T.astype(BF)
-            grads[18 + tap] = (acc_u[top:top + ch, left:left + ch] * scale).astype(BF)
+            put(tap, (acc_d[top:top + ch, left:left + ch] * scale).T)
+            put(9 + tap, (acc_m[k * ch:(k + 1) * ch, r * ch:(r + 1) * ch] * scale).T)
+            put(18 + tap, acc_u[top:top + ch, left:left + ch] * scale)
+    rest = grads.shape[1] - 27 * part
+    if rest:
+        grads[:, 27 * part:, :] = jnp.zeros((2, rest, ch), BF)
 
     def up_step(t, _):
         i = t * n_up
@@ -211,58 +249,199 @@
         def rows2(at, n):
             q = t * (n_up // 2)
             return s2[pl.ds(q, n // 2 + 1)].reshape(n + 2, wide, 2 * ch)[at + 1:at + 1 + n]
-        for rows, base, dst, weight in ((rows1, f, out, bu), (rows2, c, gout, bf)):
+        for rows, base, dst, weight in ((rows1, raw_f, out, bu), (rows2, raw_c, gout, bf)):
             lo, hi = flat(rows(0, n_up)), flat(rows(1, n_up))
             k = 2 * ch
             even = dot(lo, weight[k:2 * k, :])
             odd = dot(lo, weight[2 * k:, :]) + dot(hi, weight[:k, :])
             for a, v in enumerate((even, odd)):
-                v = v.reshape(n_up, wide, k) + base[pl.ds(i + 4, n_up), a].astype(F32)
-                dst[pl.ds(i, n_up), a] = v[:, EDGE:EDGE + cols].astype(BF)
+                v = v.reshape(n_up, wide, k)[:, EDGE:EDGE + cols]
+                otmp[:, a, pl.ds(0, cols, stride=2), :] = v[:, :, :ch]
+                otmp[:, a, pl.ds(1, cols, stride=2), :] = v[:, :, ch:]
+            at = pl.ds(2 * i, 2 * n_up)
+            total = base[at].astype(F32) + otmp[...].reshape(2 * n_up, full, ch)
+            dst[at] = total.astype(BF)
         return 0
 
     n_up = 8
     lax.fori_loop(0, half // n_up, up_step, 0)
 
 
-def shifted(x, axis, width, dim, periodic):
-    count = lax.axis_size(axis)
-    forward = [(i, i + 1) for i in range(count - 1)]
-    if periodic:
-        forward.append((count - 1, 0))
-    backward = [(b, a) for a, b in forward]
-    low = lax.ppermute(lax.slice_in_dim(x, x.shape[dim] - width, None, axis=dim), axis, forward)
-    high = lax.ppermute(lax.slice_in_dim(x, 0, width, axis=dim), axis, backward)
-    return low, high
+def exchange(f, c, wd, wm, wu, rows_out, cols_out, corners, w_out, packed, send, recv):
+    rows, full, ch = f.shape
+    lat, lon, core = (lax.axis_index(name) for name in ("lat", "lon", "dp"))
+    n_lat, n_lon = lax.axis_size("lat"), lax.axis_size("lon")
+    below, above = lat > 0, lat < n_lat - 1
+    west, east = lax.rem(lon + n_lon - 1, n_lon), lax.rem(lon + 1, n_lon)
+    other = 1 - core
+    barrier = pltpu.get_barrier_semaphore()
+
+    def greet(**where):
+        pl.semaphore_signal(barrier, inc=1, device_id=where, device_id_type=pl.DeviceIdType.MESH)
+
+    greet(lon=west)
+    greet(lon=east)
+    greet(dp=other)
+    for ok, to in ((below, lat - 1), (above, lat + 1)):
+        @pl.when(ok)
+        def _():
+            greet(lat=to)
+            greet(lat=to, lon=west)
+            greet(lat=to, lon=east)
+
+    for a, src in enumerate((f, c)):
+        for d, start in ((0, full - 16), (1, 0)):
+            x = src[:, start:start + 16, :].astype(F32)
+            x = x[:, 8:] if d == 0 else x[:, :8]
+            packed[d, a] = x.reshape(rows // 2, 16, ch).astype(BF)
+    part = wd.shape[2]
+    mine = pl.ds(pl.multiple_of(core * part, part), part)
+    for k, w in enumerate((wd, wm, wu)):
+        w_out[k, :, :, mine, :] = w[...]
+    for d, ok in ((0, below), (1, above)):
+        @pl.when(jnp.logical_not(ok))
+        def _():
+            rows_out[:, d] = jnp.zeros_like(rows_out[:, d])
+            corners[d] = jnp.zeros_like(corners[d])
+
+    pl.semaphore_wait(barrier, 3 + 3 * below.astype(jnp.int32) + 3 * above.astype(jnp.int32))
+
+    copies = []
+
+    def remote(src, dst, sends, gets, **where):
+        i = len(copies)
+        copies.append((pltpu.make_async_remote_copy(
+            src_ref=src, dst_ref=dst, send_sem=send.at[i], recv_sem=recv.at[i],
+            device_id=where, device_id_type=pl.DeviceIdType.MESH), sends, gets))
+
+    for d, to in ((0, east), (1, west)):
+        remote(packed.at[d], cols_out.at[d], None, None, lon=to)
+    for d, to, sends, gets in ((0, lat + 1, above, below), (1, lat - 1, below, above)):
+        begin = rows - 8 if d == 0 else 0
+        for a, src in enumerate((f, c)):
+            remote(src.at[pl.ds(begin, 8)], rows_out.at[a, d], sends, gets, lat=to)
+        for e, side in ((0, east), (1, west)):
+            remote(packed.at[e, :, pl.ds(begin // 2, 4)], corners.at[d, e], sends, gets, lat=to, lon=side)
+    for k, w in enumerate((wd, wm, wu)):
+        remote(w, w_out.at[k, :, :, mine, :], None, None, dp=other)
+
+    def under(condition, act):
+        if condition is None:
+            act()
+        else:
+            pl.when(condition)(act)
+
+    for copy, sends, _ in copies:
+        under(sends, copy.start)
+    for copy, sends, gets in copies:
+        under(sends, copy.wait_send)
+        under(gets, copy.wait_recv)
+
+
+def reduce(g, down, mid, up, got, st1, acc1, r2, st2, acc2, r3, whole, send, recv):
+    lat, lon, core = (lax.axis_index(name) for name in ("lat", "lon", "dp"))
+    n_lat, n_lon = lax.axis_size("lat"), lax.axis_size("lon")
+    other = 1 - core
+    share, piece = r2.shape[1], r3.shape[1]
+    east = [lax.rem(lon + k, n_lon) for k in range(1, n_lon)]
+    north = [lax.rem(lat + k, n_lat) for k in range(1, n_lat)]
+    barrier = pltpu.get_barrier_semaphore()
+    peers = [dict(dp=other)] + [dict(lon=p) for p in east] + [dict(lat=p) for p in north]
+    for where in peers:
+        pl.semaphore_signal(barrier, inc=1, device_id=where, device_id_type=pl.DeviceIdType.MESH)
+    pl.semaphore_wait(barrier, len(peers))
+    used = [0]
+
+    def remote(src, dst, **where):
+        i = used[0]
+        used[0] += 1
+        copy = pltpu.make_async_remote_copy(
+            src_ref=src, dst_ref=dst, send_sem=send.at[i], recv_sem=recv.at[i],
+            device_id=where, device_id_type=pl.DeviceIdType.MESH)
+        copy.start()
+        return copy
+
+    def at(index, size):
+        return pl.ds(pl.multiple_of(index * size, 16), size)
+
+    remote(g.at[other], got, dp=other).wait()
+    total = g[core].astype(F32) + got[...].astype(F32)
+    acc1[...] = total
+    st1[...] = total.astype(BF)
+    copies = [remote(st1.at[at(p, share)], r2.at[k], lon=p) for k, p in enumerate(east)]
+    for copy in copies:
+        copy.wait()
+    total = acc1[at(lon, share)]
+    for k in range(n_lon - 1):
+        total = total + r2[k].astype(F32)
+    acc2[...] = total
+    st2[...] = total.astype(BF)
+    copies = [remote(st2.at[at(p, piece)], r3.at[k], lat=p) for k, p in enumerate(north)]
+    for copy in copies:
+        copy.wait()
+    total = acc2[at(lat, piece)]
+    for k in range(n_lat - 1):
+        total = total + r3[k].astype(F32)
+    own = pl.ds(pl.multiple_of(lon * share + lat * piece, 16), piece)
+    whole[own] = total.astype(BF)
+    copies = [remote(whole.at[own], whole.at[own], lat=p) for p in north]
+    for copy in copies:
+        copy.wait()
+    band = at(lon, share)
+    copies = [remote(whole.at[band], whole.at[band], lon=p) for p in east]
+    for copy in copies:
+        copy.wait()
+    n = down.shape[0]
+    for k, dst in enumerate((down, mid, up)):
+        dst[...] = whole[k * n:(k + 1) * n].astype(F32)
 
 
 def body(fields, down_weight, mid_weight, up_weight, cotangent):
     _, rows, full, ch = fields.shape
     half, cols = rows // 2, full // 2
     wide = cols + 2 * EDGE
-    weights = jnp.stack([down_weight, mid_weight, up_weight])
-    weights = lax.all_gather(weights, "dp", axis=3, tiled=True)
-    cells = (lax.axis_size("dp") * rows * lax.axis_size("lat") * full * lax.axis_size("lon"))
+    n_lat, n_lon = lax.axis_size("lat"), lax.axis_size("lon")
+    cells = lax.axis_size("dp") * rows * n_lat * full * n_lon
     scale = 1.0 / math.sqrt(cells)
-    x = jnp.stack([fields[0], cotangent[0]]).reshape(2, rows, cols, 2 * ch)
-    low, high = shifted(x, "lat", 8, 1, False)
-    tall = jnp.concatenate([low, x, high, jnp.zeros((2, 2, cols, 2 * ch), BF)], axis=1)
-    low, high = shifted(tall, "lon", 4, 2, True)
-    gap = jnp.zeros((2, rows + 18, EDGE - 4, 2 * ch), BF)
-    whole = jnp.concatenate([gap, low, tall, high, gap], axis=2)
-    whole = whole.reshape(2, half + 9, 2, wide, 2 * ch)
     k = 2 * ch
     vm = pl.BlockSpec(memory_space=pltpu.VMEM)
-    out, gout, grads = pl.pallas_call(
-        functools.partial(compute, half, scale),
+
+    def sds(shape, dtype=BF):
+        return jax.ShapeDtypeStruct(shape, dtype)
+
+    f, c = fields[0], cotangent[0]
+    halo = pl.pallas_call(
+        exchange,
         out_shape=(
-            jax.ShapeDtypeStruct((half, 2, cols, k), BF),
-            jax.ShapeDtypeStruct((half, 2, cols, k), BF),
-            jax.ShapeDtypeStruct((27, ch, ch), BF),
+            sds((2, 2, 8, full, ch)),
+            sds((2, 2, half, 16, ch)),
+            sds((2, 2, 2, 4, 16, ch)),
+            sds((3, 3, 3, ch, ch)),
         ),
         in_specs=[vm] * 5,
+        out_specs=(vm,) * 4,
+        scratch_shapes=[
+            pltpu.VMEM((2, 2, half, 16, ch), BF),
+            pltpu.SemaphoreType.DMA((13,)),
+            pltpu.SemaphoreType.DMA((13,)),
+        ],
+        compiler_params=pltpu.CompilerParams(
+            collective_id=0, has_side_effects=True, vmem_limit_bytes=40 << 20),
+    )(f, c, down_weight, mid_weight, up_weight)
+
+    unit = n_lat * n_lon * 16
+    taps = 27 * (ch // 2)
+    padded = -(-taps // unit) * unit
+    out, gout, grads = pl.pallas_call(
+        functools.partial(compute, scale),
+        out_shape=(sds((rows, full, ch)), sds((rows, full, ch)), sds((2, padded, ch))),
+        in_specs=[vm] * 6,
         out_specs=(vm, vm, vm),
         scratch_shapes=[
+            pltpu.VMEM((half + 9, 2, wide, k), BF),
+            pltpu.VMEM((half + 9, 2, wide, k), BF),
+            pltpu.VMEM((8, full + 4 * HALO, ch), F32),
+            pltpu.VMEM((8, 2, full, ch), F32),
             pltpu.VMEM((3 * k, k), BF),
             pltpu.VMEM((3 * k, k), BF),
             pltpu.VMEM((2 * k, 3 * k), BF),
@@ -278,18 +457,32 @@
             pltpu.VMEM((3 * ch, 3 * ch), F32),
             pltpu.VMEM((k, 3 * k), F32),
         ],
-        compiler_params=pltpu.CompilerParams(vmem_limit_bytes=50 << 20),
-    )(whole[0], whole[1], weights[0], weights[1], weights[2])
-    mine = lax.psum_scatter(grads, "dp", scatter_dimension=1, tiled=True)
-    total = lax.psum(mine.astype(F32), ("lat", "lon"))
-    total = total.reshape(3, 3, 3, ch // lax.axis_size("dp"), ch)
-    return (
-        out.reshape(1, rows, full, ch),
-        gout.reshape(1, rows, full, ch),
-        total[0],
-        total[1],
-        total[2],
-    )
+        compiler_params=pltpu.CompilerParams(vmem_limit_bytes=56 << 20),
+    )(f, c, *halo)
+
+    share, piece = padded // n_lon, padded // (n_lon * n_lat)
+    count = 1 + 2 * (n_lon - 1) + 2 * (n_lat - 1)
+    terms = pl.pallas_call(
+        reduce,
+        out_shape=(sds((taps // 3, ch), F32),) * 3,
+        in_specs=[vm],
+        out_specs=(vm,) * 3,
+        scratch_shapes=[
+            pltpu.VMEM((padded, ch), BF),
+            pltpu.VMEM((padded, ch), BF),
+            pltpu.VMEM((padded, ch), F32),
+            pltpu.VMEM((n_lon - 1, share, ch), BF),
+            pltpu.VMEM((share, ch), BF),
+            pltpu.VMEM((share, ch), F32),
+            pltpu.VMEM((n_lat - 1, piece, ch), BF),
+            pltpu.VMEM((padded, ch), BF),
+            pltpu.SemaphoreType.DMA((count,)),
+            pltpu.SemaphoreType.DMA((count,)),
+        ],
+        compiler_params=pltpu.CompilerParams(
+            collective_id=1, has_side_effects=True, vmem_limit_bytes=40 << 20),
+    )(grads)
+    return (out[None], gout[None]) + tuple(t.reshape(3, 3, ch // 2, ch) for t in terms)
 
 
 def solution(mesh):

time: 236 us -> 88.9 us (0.38)
  blocking collectives: 91 us -> 0 us
  Pallas kernels: 23.9 us -> 75.1 us
  local copies, waits for them, and re-layouts: 58.7 us -> 12.9 us
  waiting for transfers between devices: 27.8 us -> 0 us
  between operations: 14.1 us -> 0.67 us
  other arithmetic: 10.1 us -> 0 us
  starting transfers between devices: 9.27 us -> 0 us
    psum x1 -> x0, blocking collectives: 88.6 us -> none  [body(): total = lax.psum(mine.astype(F32), ('lat', 'lon'))]
    pallas_call x1 -> x3, Pallas kernels: 23.9 us -> 75.1 us  [the longest x1 27.2 us: body(): pl.pallas_call(reduce, out_shape=(sds((taps // 3, ch), F32),) * 3, in_spe...]
    concatenate x2 -> x0, local copies, waits for them, and re-layouts: 33.8 us -> none  [the longest x1 33.7 us: body(): whole = jnp.concatenate([gap, low, tall, high, gap], axis=2)]
    ppermute x4 -> x0, waiting for transfers between devices: 27.8 us -> none  [the longest x2 17.4 us: shifted(): lax.ppermute(lax.slice_in_dim(x, x.shape[dim] - width, None, axis=dim), a...]
    reshape x3 -> x0, local copies, waits for them, and re-layouts: 16.7 us -> none  [the longest x1 8.61 us: body(): x = jnp.stack([fields[0], cotangent[0]]).reshape(2, rows, cols, 2 * ch)]
    unnamed x10 -> x23, local copies, waits for them, and re-layouts: 0.02 us -> 12.9 us
    ppermute x4 -> x0, starting transfers between devices: 9.23 us -> none  [the longest x2 6.5 us: shifted(): lax.ppermute(lax.slice_in_dim(x, x.shape[dim] - width, None, axis=dim), a...]
    slice x4 -> x0, local copies, waits for them, and re-layouts: 8.04 us -> none  [the longest x1 5.53 us: body(): whole[1]]
  transfers between devices with their start and end apart: 5 -> 0, of which waited for: 4 -> 0; matrix products, arithmetic and copies ran while one was open for 4% -> 0% of each run, Pallas kernels for 0% -> 0%
where the time goes in v1:
time: 88.9 us; the launch traced here: 88.6 us
  Pallas kernels  75.1 us (84%)
  local copies, waits for them, and re-layouts  12.9 us (15%)
    pallas_call x1, Pallas kernels, body(): pl.pallas_call(reduce, out_shape=(sds((taps // 3, ch), F32),) * 3, in_spe...  27.2 us
    pallas_call x1, Pallas kernels, body(): pl.pallas_call(functools.partial(compute, scale), out_shape=(sds((rows, f...  26.3 us
    pallas_call x1, Pallas kernels, body(): pl.pallas_call(exchange, out_shape=(sds((2, 2, 8, full, ch)), sds((2, 2,...  21.5 us
    unnamed x23, local copies, waits for them, and re-layouts  12.9 us

profile of v1, /device:TPU:0, one launch (start us, length us, event | category | flops | bytes accessed | tf_op | source)
XLA Modules:
  0.0 88.6 jit_solution(1761659209279610243)
XLA Ops:
  0.6 0.0 copy-start
  0.6 1.7 %copy-done = bf16[1,80,128,128]{3,2,1,0:T(8,128)(2,1)S(1)} copy-done((bf16[1,80,128,128]{3,2,1,0:T(8,128)(2,1)S(1)}, bf16[1,80,128,128]{3,2,1,0:T(8,128)(2,1)}, u32[]{:S(2)}) %copy-start) | copy-done | bytes 2621464
  2.4 0.0 copy-start.1
  2.4 1.7 %copy-done.1 = bf16[1,80,128,128]{3,2,1,0:T(8,128)(2,1)S(1)} copy-done((bf16[1,80,128,128]{3,2,1,0:T(8,128)(2,1)S(1)}, bf16[1,80,128,128]{3,2,1,0:T(8,128)(2,1)}, u32[]{:S(2)}) %copy-start.1) | copy-done | bytes 2621464
  4.1 0.0 copy-start.6
  4.1 0.9 %copy-done.6 = bf16[3,3,64,128]{3,2,1,0:T(8,128)(2,1)S(1)} copy-done((bf16[3,3,64,128]{3,2,1,0:T(8,128)(2,1)S(1)}, bf16[3,3,64,128]{3,2,1,0:T(8,128)(2,1)}, u32[]{:S(2)}) %copy-start.6) | copy-done | bytes 147480
  5.0 0.0 copy-start.7
  5.0 0.9 %copy-done.7 = bf16[3,3,64,128]{3,2,1,0:T(8,128)(2,1)S(1)} copy-done((bf16[3,3,64,128]{3,2,1,0:T(8,128)(2,1)S(1)}, bf16[3,3,64,128]{3,2,1,0:T(8,128)(2,1)}, u32[]{:S(2)}) %copy-start.7) | copy-done | bytes 147480
  5.9 0.0 copy-start.8
  5.9 0.9 %copy-done.8 = bf16[3,3,64,128]{3,2,1,0:T(8,128)(2,1)S(1)} copy-done((bf16[3,3,64,128]{3,2,1,0:T(8,128)(2,1)S(1)}, bf16[3,3,64,128]{3,2,1,0:T(8,128)(2,1)}, u32[]{:S(2)}) %copy-start.8) | copy-done | bytes 147480
  6.8 21.5 %shard_map.92 = (bf16[2,2,8,128,128]{4,3,2,1,0:T(8,128)(2,1)S(1)}, bf16[2,2,40,16,128]{4,3,2,1,0:T(8,128)(2,1)S(1)}, bf16[2,2,2,4,16,128]{5,4,3,2,1,0:T(8,128)(2,1)S(1)}, bf16[3,3,3,128,128]{4,3,2,1,0:T(8,128)(2,1)S(1)}) custom-call(bf16[80,128,128]{2,1,0:T(8,128)(2,1)S(1)} %bitcast.8, bf16[80,128,128]{2,1,0:T(8,128)(2,1)S(1)} %bitcast.10, ...), custom_call_target="tpu_custom_call" | custom-call | tf_op jit(solution)/shard_map/pallas_call | solution.py:413
  28.4 0.0 copy-start.2
  28.4 1.0 %copy-done.2 = bf16[2,2,8,128,128]{4,3,2,1,0:T(8,128)(2,1)} copy-done((bf16[2,2,8,128,128]{4,3,2,1,0:T(8,128)(2,1)}, bf16[2,2,8,128,128]{4,3,2,1,0:T(8,128)(2,1)S(1)}, u32[]{:S(2)}) %copy-start.2) | copy-done | bytes 1048600
  29.4 0.0 copy-start.4
  29.4 0.9 %copy-done.4 = bf16[3,3,3,128,128]{4,3,2,1,0:T(8,128)(2,1)} copy-done((bf16[3,3,3,128,128]{4,3,2,1,0:T(8,128)(2,1)}, bf16[3,3,3,128,128]{4,3,2,1,0:T(8,128)(2,1)S(1)}, u32[]{:S(2)}) %copy-start.4) | copy-done | bytes 884760
  30.3 0.0 copy-start.5
  30.3 0.8 copy-done.5
  31.1 0.7 copy-done.9
  31.8 26.3 %shard_map.93 = (bf16[80,128,128]{2,1,0:T(8,128)(2,1)}, bf16[80,128,128]{2,1,0:T(8,128)(2,1)}, bf16[2,1792,128]{2,1,0:T(8,128)(2,1)}) custom-call(bf16[80,128,128]{2,1,0:T(8,128)(2,1)} %bitcast.7, bf16[80,128,128]{2,1,0:T(8,128)(2,1)} %bitcast.9, bf16[2,2,8,128,128]{4,3,2,1,0:T(8,128)(2,1)} %copy-done.2, bf16[2,2,40,16,128]{4,3,2,1,0:T(8,128)(2,1)} %copy-done.5, ...), custom_call_target="tpu_custom_call" | custom-call | tf_op jit(solution)/shard_map/pallas_call | solution.py:435
  58.1 1.2 %copy-done.3 = bf16[2,1792,128]{2,1,0:T(8,128)(2,1)S(1)} copy-done((bf16[2,1792,128]{2,1,0:T(8,128)(2,1)S(1)}, bf16[2,1792,128]{2,1,0:T(8,128)(2,1)}, u32[]{:S(2)}) %copy-start.3) | copy-done | bytes 917528
  59.2 27.2 %shard_map.94 = (f32[576,128]{1,0:T(8,128)S(1)}, f32[576,128]{1,0:T(8,128)S(1)}, f32[576,128]{1,0:T(8,128)S(1)}) custom-call(bf16[2,1792,128]{2,1,0:T(8,128)(2,1)S(1)} %copy-done.3), custom_call_target="tpu_custom_call" | custom-call | tf_op jit(solution)/shard_map/pallas_call | solution.py:465
  86.5 0.7 copy.13
  87.2 0.7 copy.14
  87.9 0.7 copy.15
  (2 shorter events, 0.0 us)
Async XLA Ops:
  0.6 1.7 %copy-start = (bf16[1,80,128,128]{3,2,1,0:T(8,128)(2,1)S(1)}, bf16[1,80,128,128]{3,2,1,0:T(8,128)(2,1)}, u32[]{:S(2)}) copy-start(bf16[1,80,128,128]{3,2,1,0:T(8,128)(2,1)} %param.5) | copy-start | bytes 7864324
  2.4 1.7 %copy-start.1 = (bf16[1,80,128,128]{3,2,1,0:T(8,128)(2,1)S(1)}, bf16[1,80,128,128]{3,2,1,0:T(8,128)(2,1)}, u32[]{:S(2)}) copy-start(bf16[1,80,128,128]{3,2,1,0:T(8,128)(2,1)} %param.9) | copy-start | bytes 7864324
  4.1 0.9 %copy-start.6 = (bf16[3,3,64,128]{3,2,1,0:T(8,128)(2,1)S(1)}, bf16[3,3,64,128]{3,2,1,0:T(8,128)(2,1)}, u32[]{:S(2)}) copy-start(bf16[3,3,64,128]{3,2,1,0:T(8,128)(2,1)} %wd.1) | copy-start | bytes 442372
  5.0 0.9 %copy-start.7 = (bf16[3,3,64,128]{3,2,1,0:T(8,128)(2,1)S(1)}, bf16[3,3,64,128]{3,2,1,0:T(8,128)(2,1)}, u32[]{:S(2)}) copy-start(bf16[3,3,64,128]{3,2,1,0:T(8,128)(2,1)} %wm.1) | copy-start | bytes 442372
  5.9 0.9 %copy-start.8 = (bf16[3,3,64,128]{3,2,1,0:T(8,128)(2,1)S(1)}, bf16[3,3,64,128]{3,2,1,0:T(8,128)(2,1)}, u32[]{:S(2)}) copy-start(bf16[3,3,64,128]{3,2,1,0:T(8,128)(2,1)} %wu.1) | copy-start | bytes 442372
  28.4 1.0 %copy-start.2 = (bf16[2,2,8,128,128]{4,3,2,1,0:T(8,128)(2,1)}, bf16[2,2,8,128,128]{4,3,2,1,0:T(8,128)(2,1)S(1)}, u32[]{:S(2)}) copy-start(bf16[2,2,8,128,128]{4,3,2,1,0:T(8,128)(2,1)S(1)} %get-tuple-element.15.rows_in) | copy-start | bytes 3145732
  29.4 0.9 %copy-start.4 = (bf16[3,3,3,128,128]{4,3,2,1,0:T(8,128)(2,1)}, bf16[3,3,3,128,128]{4,3,2,1,0:T(8,128)(2,1)S(1)}, u32[]{:S(2)}) copy-start(bf16[3,3,3,128,128]{4,3,2,1,0:T(8,128)(2,1)S(1)} %get-tuple-element.18.w_in) | copy-start | bytes 2654212
  30.3 0.8 copy-start.5
  31.1 0.7 copy-start.9
  58.1 1.2 %copy-start.3 = (bf16[2,1792,128]{2,1,0:T(8,128)(2,1)S(1)}, bf16[2,1792,128]{2,1,0:T(8,128)(2,1)}, u32[]{:S(2)}) copy-start(bf16[2,1792,128]{2,1,0:T(8,128)(2,1)} %get-tuple-element.21.g) | copy-start | bytes 2752516

commit v2 on v0

v2 whole, which is shorter than its diff:
```python
import functools
import math

import jax
import jax.numpy as jnp
from jax import lax
from jax.experimental import pallas as pl
from jax.experimental.pallas import tpu as pltpu
from jax.sharding import PartitionSpec as P

EDGE = 8
HALO = 8
BF = jnp.bfloat16
F32 = jnp.float32


def dot(a, b):
    return lax.dot_general(a, b, (((1,), (0,)), ((), ())), preferred_element_type=F32)


def dot_t(a, b):
    return lax.dot_general(a, b, (((0,), (0,)), ((), ())), preferred_element_type=F32)


def rolled(x, by):
    return pltpu.roll(x, by % x.shape[0], 0)


def lanes(*parts):
    return jnp.concatenate(parts, axis=-1)


def blocks(rows):
    return jnp.concatenate([lanes(*row) for row in rows], axis=0)


def strided_block(w, r, z):
    return blocks([[w(r, 1), z], [w(r, 2), w(r, 0)]])


def spread_block(w, r, z):
    return blocks([[w(r, 1), w(r, 2)], [z, w(r, 0)]])


def paired_block(w, c, z):
    return blocks([[w(0, c), z], [w(1, c), w(0, c)], [w(2, c), w(1, c)], [z, w(2, c)]])


def flat(x):
    return x.reshape(x.shape[0] * x.shape[1], x.shape[2])


def level(scale, f_in, c_in, wd_in, wm_in, wu_in, out, gout, down_out, mid_out, up_out,
          raw_f, raw_c, rows_in, low_in, high_in, pair_in, low_at, high_at, pair_at,
          low_out, high_out, pair_out, w_in, local, send, recv,
          f, c, tmp, otmp, bd, bg, bm, bn, bu, bf, dp, gps, gpp, s1, s2, acc_u, acc_m, acc_d,
          *sums):
    rows = raw_f.shape[0]
    half = rows // 2
    wd, wm, wu = w_in.at[0], w_in.at[1], w_in.at[2]
    wide = f.shape[2]
    ch = f.shape[3] // 2
    cols = wide - 2 * EDGE
    z = jnp.zeros((ch, ch), BF)
    lat = lax.axis_index("lat")
    lon, core = lax.axis_index("lon"), lax.axis_index("dp")
    n_lat, n_lon = lax.axis_size("lat"), lax.axis_size("lon")
    other = 1 - core
    below, above = lat > 0, lat < n_lat - 1
    low = jnp.where(below, -(1 << 20), 0)
    high = jnp.where(above, 1 << 20, half)
    full = 2 * cols
    east = [lax.rem(lon + k, n_lon) for k in range(1, n_lon)]
    north = [lax.rem(lat + k, n_lat) for k in range(1, n_lat)]

    rows_in[...] = jnp.zeros_like(rows_in)
    for ref in (low_at, high_at, pair_at):
        ref[...] = jnp.zeros_like(ref)

    barrier = pltpu.get_barrier_semaphore()

    def greet(**where):
        pl.semaphore_signal(barrier, inc=1, device_id=where, device_id_type=pl.DeviceIdType.MESH)

    greet(dp=other)
    for p in east:
        greet(lon=p)
    for p in north:
        greet(lat=p)
    for ok, to in ((below, lat - 1), (above, lat + 1)):
        @pl.when(ok)
        def _(to=to):
            greet(lat=to, lon=east[0])
            greet(lat=to, lon=east[-1])

    part = ch // 2
    mine = pl.ds(pl.multiple_of(core * part, part), part)
    loads = [pltpu.make_async_copy(f_in, raw_f, local.at[0]), pltpu.make_async_copy(c_in, raw_c, local.at[1])]
    for i, w in enumerate((wd_in, wm_in, wu_in)):
        loads.append(pltpu.make_async_copy(w, w_in.at[i, :, :, mine, :], local.at[2 + i]))
    for load in loads:
        load.start()
    pl.semaphore_wait(barrier, n_lon + n_lat - 1 + 2 * below.astype(jnp.int32) + 2 * above.astype(jnp.int32))

    used = [0]

    def remote(src, dst, **where):
        i = used[0]
        used[0] += 1
        return pltpu.make_async_remote_copy(
            src_ref=src, dst_ref=dst, send_sem=send.at[i], recv_sem=recv.at[i],
            device_id=where, device_id_type=pl.DeviceIdType.MESH)

    def under(condition, act):
        if condition is None:
            act()
        else:
            pl.when(condition)(act)

    halos = []
    for k, w in enumerate((wd_in, wm_in, wu_in)):
        halos.append((remote(w, w_in.at[k, :, :, mine, :], dp=other), None, None))
    for a, src in enumerate((f_in, c_in)):
        n0, n1 = (5, 6) if a == 0 else (3, 4)
        halos.append((remote(src.at[pl.ds(rows - n0, n0)], rows_in.at[a, 0, pl.ds(8 - n0, n0)], lat=lat + 1), above, below))
        halos.append((remote(src.at[pl.ds(0, n1)], rows_in.at[a, 1, pl.ds(0, n1)], lat=lat - 1), below, above))
    early = len(halos)
    for copy, sends, _ in halos:
        under(sends, copy.start)

    loads[0].wait()
    loads[1].wait()

    def slots(n):
        return lax.broadcasted_iota(jnp.int32, (n, HALO, ch), 1)

    x_f = raw_f[:, full - 16:, :].astype(F32)[:, 8:]
    x_c = raw_c[:, full - 16:, :].astype(F32)[:, 8:]
    x = jnp.where(slots(rows) < 5, pltpu.roll(x_f, 5, 1), x_c)
    low_out[...] = x.reshape(half, 16, ch).astype(BF)
    high_out[...] = raw_f[:, :16, :].astype(F32)[:, :8].reshape(half, 16, ch).astype(BF)
    x = raw_c[:, :16, :].astype(F32)[:, :8].reshape(half, 2, HALO, ch)
    x = jnp.where(slots(half) < 4, x[:, 0], pltpu.roll(x[:, 1], 4, 1))
    pair_out[...] = x.reshape(half // 2, 16, ch).astype(BF)

    halos.append((remote(low_out, low_in, lon=east[0]), None, None))
    halos.append((remote(high_out, high_in, lon=east[-1]), None, None))
    halos.append((remote(pair_out, pair_in, lon=east[-1]), None, None))
    for d, to, sends, gets in ((0, lat + 1, above, below), (1, lat - 1, below, above)):
        begin = half - 4 if d == 0 else 0
        here = pl.ds(begin, 4)
        halos.append((remote(low_out.at[here], low_at.at[d], lat=to, lon=east[0]), sends, gets))
        halos.append((remote(high_out.at[here], high_at.at[d], lat=to, lon=east[-1]), sends, gets))
        here = pl.ds(begin // 2, 2)
        halos.append((remote(pair_out.at[here], pair_at.at[d], lat=to, lon=east[-1]), sends, gets))
    for copy, sends, _ in halos[early:]:
        under(sends, copy.start)
    for load in loads[2:]:
        load.wait()

    def landed(part_of):
        for copy, sends, gets in part_of:
            under(sends, copy.wait_send)
            under(gets, copy.wait_recv)

    def plain(ref):
        return lambda r, k: ref[r, k]

    def turned(ref):
        return lambda r, k: ref[r, k].T

    def flipped(ref):
        return lambda r, k: ref[2 - r, 2 - k].T

    def inside(at):
        return jnp.logical_and(at >= low, at < high)

    def pair_mask(n, base):
        shape = (n, wide, 2 * ch)
        rows = (base + 2 * lax.broadcasted_iota(jnp.int32, shape, 0)
                + (lax.broadcasted_iota(jnp.int32, shape, 2) >= ch).astype(jnp.int32))
        return inside(rows)

    def strided(src, start, n, weight):
        x0 = src[pl.ds(start, n), 1]
        x1 = src[pl.ds(start + 1, n), 0]
        x2 = src[pl.ds(start + 1, n), 1]
        acc = dot(flat(lanes(x0, x1, x2)), weight[...])
        return acc[:, :ch] + rolled(acc[:, ch:], 1)

    def to_pairs(x, n):
        x = x.reshape(n, 2, wide, ch)
        return lanes(x[:, 0], x[:, 1])

    def same(src, start, n, weight):
        acc = dot(flat(lanes(src[pl.ds(start, n)], src[pl.ds(start + 1, n)])), weight[...])
        k = 2 * ch
        total = rolled(acc[:, :k], 1) + acc[:, k:2 * k] + rolled(acc[:, 2 * k:], -1)
        return total

    side = jnp.zeros((8, 2 * HALO, ch), F32)
    tmp[:, 0:2 * HALO, :] = side
    tmp[:, full + 2 * HALO:, :] = side

    def lay(dst, pair, middle):
        tmp[:, 2 * HALO:2 * HALO + full, :] = middle.astype(F32)
        even = tmp[:, pl.ds(0, wide, stride=2), :]
        odd = tmp[:, pl.ds(1, wide, stride=2), :]
        dst[pl.ds(pair, 4)] = lanes(even, odd).astype(BF).reshape(4, 2, wide, 2 * ch)

    def lay_step(t, _):
        lay(f, 4 * t + 4, raw_f[pl.ds(8 * t, 8)])
        lay(c, 4 * t + 4, raw_c[pl.ds(8 * t, 8)])
        return 0

    lax.fori_loop(0, half // 4, lay_step, 0)
    for dst in (f, c):
        dst[half + 8] = jnp.zeros((2, wide, 2 * ch), BF)

    landed(halos[:3])
    for r in range(3):
        at = pl.ds(2 * ch * r, 2 * ch)
        bd[at, :] = strided_block(plain(wd), r, z)
        bg[at, :] = strided_block(turned(wu), r, z)
        bu[at, :] = spread_block(plain(wu), r, z)
        bf[at, :] = spread_block(turned(wd), r, z)
        bm[:, at] = paired_block(plain(wm), r, z)
        bn[:, at] = paired_block(flipped(wm), r, z)

    landed(halos[3:early])
    for a, dst in enumerate((f, c)):
        lay(dst, 0, rows_in[a, 0])
        lay(dst, half + 4, rows_in[a, 1])

    landed(halos[early:])

    def edge(dst, pair, lower, upper):
        tmp[:, HALO:2 * HALO, :] = lower
        tmp[:, 3 * HALO:4 * HALO, :] = jnp.zeros_like(lower)
        tmp[:, 2 * HALO:3 * HALO, :] = upper
        at = pl.ds(pair, 4)
        new = lanes(tmp[:, pl.ds(0, HALO, stride=2), :], tmp[:, pl.ds(1, HALO, stride=2), :])
        old = dst[at, :, 0:16, :].astype(F32).reshape(8, 16, 2 * ch)
        dst[at, :, 0:16, :] = jnp.concatenate([new, old[:, 8:]], axis=1).astype(BF).reshape(4, 2, 16, 2 * ch)
        new = lanes(tmp[:, pl.ds(2 * HALO, HALO, stride=2), :], tmp[:, pl.ds(2 * HALO + 1, HALO, stride=2), :])
        old = dst[at, :, wide - 16:, :].astype(F32).reshape(8, 16, 2 * ch)
        dst[at, :, wide - 16:, :] = jnp.concatenate([old[:, :8], new], axis=1).astype(BF).reshape(4, 2, 16, 2 * ch)

    def edges(pair, lower, upper, paired):
        slot = slots(8)
        z8 = jnp.zeros((8, HALO, ch), F32)
        lower = lower.astype(F32).reshape(8, HALO, ch)
        upper = upper.astype(F32).reshape(8, HALO, ch)
        paired = paired.astype(F32).reshape(4, 1, HALO, ch)
        paired = jnp.concatenate([paired, pltpu.roll(paired.reshape(4, HALO, ch), 4, 1)[:, None]], axis=1)
        paired = paired.reshape(8, HALO, ch)
        edge(f, pair, jnp.where(slot >= 3, pltpu.roll(lower, 3, 1), z8), upper)
        edge(c, pair, jnp.where(slot >= 5, lower, z8), jnp.where(slot < 4, paired, z8))

    tmp[:, 0:HALO, :] = jnp.zeros((8, HALO, ch), F32)

    def edge_step(t, _):
        at = pl.ds(4 * t, 4)
        edges(4 * t + 4, low_in[at], high_in[at], pair_in[pl.ds(2 * t, 2)])
        return 0

    lax.fori_loop(0, half // 4, edge_step, 0)
    edges(0, low_at[0], high_at[0], pair_at[0])
    edges(half + 4, low_at[1], high_at[1], pair_at[1])

    pairs = (half + 8) // 2
    nd = 6 if pairs % 6 == 0 else 1

    def down_step(t, _):
        q = t * nd
        v = strided(f, 2 * q, 2 * nd, bd)
        v = to_pairs(v, nd)
        dp[pl.ds(q, nd)] = jnp.where(pair_mask(nd, 2 * q - 3), v, 0.0).astype(BF)
        return 0

    lax.fori_loop(0, pairs // nd, down_step, 0)

    def shifted_rows(dst, start, n, v):
        nxt = rolled(v, -1)
        for a in range(2):
            half_lanes = slice(a * ch, (a + 1) * ch)
            piece = lanes(v[:, half_lanes], nxt[:, half_lanes]).astype(BF)
            dst[pl.ds(start, n), a] = piece.reshape(n, wide, 2 * ch)

    pairs_mid = (half + 4) // 2
    nm = 11 if pairs_mid % 11 == 0 else 1

    def mid_step(t, _):
        p = t * nm
        pre = same(dp, p, nm, bm)
        g = strided(c, 2 * p + 1, 2 * nm, bg)
        g = flat(to_pairs(g, nm))
        sig = jax.nn.sigmoid(pre)
        ok = flat(pair_mask(nm, 2 * p - 2))
        mid = jnp.where(ok, pre * sig, 0.0)
        gp = jnp.where(ok, g * sig * (1.0 + pre * (1.0 - sig)), 0.0)
        shifted_rows(s1, p, nm, mid)
        gpp[pl.ds(p, nm)] = gp.astype(BF).reshape(nm, wide, 2 * ch)
        place = lax.broadcasted_iota(jnp.int32, (nm, wide, 2 * ch), 1)
        own = flat(jnp.logical_and(place >= EDGE, place < EDGE + cols))
        gm = jnp.where(own, gp, 0.0)
        after, before = rolled(gm, -1), rolled(gm, 1)
        for a in range(2):
            k = slice(a * ch, (a + 1) * ch)
            piece = lanes(after[:, k], gm[:, k], before[:, k]).astype(BF)
            gps[pl.ds(p, nm), a] = piece.reshape(nm, wide, 3 * ch)
        return 0

    lax.fori_loop(0, pairs_mid // nm, mid_step, 0)

    acc_u[...] = jnp.zeros_like(acc_u)
    acc_m[...] = jnp.zeros_like(acc_m)
    acc_d[...] = jnp.zeros_like(acc_d)
    place = lax.broadcasted_iota(jnp.int32, (wide, 2 * ch), 0)
    place = place + (lax.broadcasted_iota(jnp.int32, (wide, 2 * ch), 1) >= ch).astype(jnp.int32)
    own = jnp.logical_and(place >= EDGE, place < EDGE + cols).astype(F32).astype(BF)[None]
    step = 4

    def taps(src, i, n):
        return flat(lanes(src[pl.ds(i + 3, n), 1], src[pl.ds(i + 4, n), 0], src[pl.ds(i + 4, n), 1]))

    def first_grads(t, _):
        p = t * step
        n = 2 * step
        m = s1[pl.ds(p + 1, step)].reshape(n, wide, 2 * ch) * own
        acc_u[...] += dot_t(flat(m), taps(c, 2 * p, n))
        d0, d1 = dp[pl.ds(p + 1, step)], dp[pl.ds(p + 2, step)]
        acc_m[...] += (
            dot_t(flat(gps[pl.ds(p + 1, step), 0]), flat(lanes(d0, d1[:, :, :ch])))
            + dot_t(flat(gps[pl.ds(p + 1, step), 1]), flat(lanes(d0[:, :, ch:], d1)))
        )
        return 0

    def last_grads(t, _):
        p = t * step
        n = 2 * step
        ga = s2[pl.ds(p, step + 1)].reshape(2 * step + 2, wide, 2 * ch)[1:1 + n] * own
        acc_d[...] += dot_t(flat(ga), taps(f, 2 * p, n))
        return 0

    def put(grads, tap, value):
        value = value.astype(BF)
        for h in range(2):
            grads[h, tap * part:(tap + 1) * part, :] = value[h * part:(h + 1) * part]

    def clear(grads, count):
        rest = grads.shape[1] - count * part
        if rest:
            grads[:, count * part:, :] = jnp.zeros((2, rest, ch), BF)

    batch_a = total_of(remote, sums[:8], (mid_out, up_out), lat, lon, core, north, east)
    batch_b = total_of(remote, sums[8:], (down_out,), lat, lon, core, north, east)

    lax.fori_loop(0, half // (2 * step), first_grads, 0)
    where = [(r, k, ch if k == 0 else 0, 2 * ch * r + (0 if k == 1 else ch)) for r in range(3) for k in range(3)]
    for r, k, top, left in where:
        tap = 3 * r + k
        put(sums[0], tap, (acc_m[k * ch:(k + 1) * ch, r * ch:(r + 1) * ch] * scale).T)
        put(sums[0], 9 + tap, acc_u[top:top + ch, left:left + ch] * scale)
    clear(sums[0], 18)
    next(batch_a)

    pairs_gd = (half + 2) // 2
    ng = 7 if pairs_gd % 7 == 0 else 1

    def gd_step(t, _):
        q = t * ng
        v = same(gpp, q, ng, bn)
        v = jnp.where(flat(pair_mask(ng, 2 * q - 1)), v, 0.0)
        shifted_rows(s2, q, ng, v)
        return 0

    lax.fori_loop(0, 1, gd_step, 0)
    next(batch_a)
    lax.fori_loop(1, pairs_gd // ng, gd_step, 0)
    lax.fori_loop(0, half // (2 * step), last_grads, 0)
    for r, k, top, left in where:
        put(sums[8], 3 * r + k, (acc_d[top:top + ch, left:left + ch] * scale).T)
    clear(sums[8], 9)
    next(batch_b)
    next(batch_a)

    def up_step(t, _):
        i = t * n_up
        def rows1(at, n):
            q = t * (n_up // 2) + 1
            return s1[pl.ds(q, n // 2 + 1)].reshape(n + 2, wide, 2 * ch)[at:at + n]
        def rows2(at, n):
            q = t * (n_up // 2)
            return s2[pl.ds(q, n // 2 + 1)].reshape(n + 2, wide, 2 * ch)[at + 1:at + 1 + n]
        for rows, base, dst, weight in ((rows1, raw_f, out, bu), (rows2, raw_c, gout, bf)):
            lo, hi = flat(rows(0, n_up)), flat(rows(1, n_up))
            k = 2 * ch
            even = dot(lo, weight[k:2 * k, :])
            odd = dot(lo, weight[2 * k:, :]) + dot(hi, weight[:k, :])
            for a, v in enumerate((even, odd)):
                v = v.reshape(n_up, wide, k)[:, EDGE:EDGE + cols]
                otmp[:, a, pl.ds(0, cols, stride=2), :] = v[:, :, :ch]
                otmp[:, a, pl.ds(1, cols, stride=2), :] = v[:, :, ch:]
            at = pl.ds(2 * i, 2 * n_up)
            total = base[at].astype(F32) + otmp[...].reshape(2 * n_up, full, ch)
            dst[at] = total.astype(BF)
        return 0

    n_up = 8
    steps = half // n_up
    cuts = [steps * i // 5 for i in range(6)]
    for i in range(5):
        lax.fori_loop(cuts[i], cuts[i + 1], up_step, 0)
        next(batch_b, None)
        next(batch_a, None)


def total_of(remote, refs, outs, lat, lon, core, north, east):
    g, got, st1, r2, st2, r3, whole, acc = refs
    share, piece = st2.shape[0], r3.shape[1]

    def at(index, size):
        return pl.ds(pl.multiple_of(index * size, 16), size)

    def begin(copies):
        for copy in copies:
            copy.start()
        return copies

    def end(copies):
        for copy in copies:
            copy.wait()

    copies = begin([remote(g.at[1 - core], got, dp=1 - core)])
    yield
    end(copies)
    total = g[core].astype(F32) + got[...].astype(F32)
    acc[...] = total
    st1[...] = total.astype(BF)
    copies = begin([remote(st1.at[at(p, share)], r2.at[k], lon=p) for k, p in enumerate(east)])
    yield
    end(copies)
    total = acc[at(lon, share)]
    for k in range(len(east)):
        total = total + r2[k].astype(F32)
    acc[0:share] = total
    st2[...] = total.astype(BF)
    copies = begin([remote(st2.at[at(p, piece)], r3.at[k], lat=p) for k, p in enumerate(north)])
    yield
    end(copies)
    total = acc[at(lat, piece)]
    for k in range(len(north)):
        total = total + r3[k].astype(F32)
    own = pl.ds(pl.multiple_of(lon * share + lat * piece, 16), piece)
    whole[own] = total.astype(BF)
    copies = begin([remote(whole.at[own], whole.at[own], lat=p) for p in north])
    yield
    end(copies)
    band = at(lon, share)
    copies = begin([remote(whole.at[band], whole.at[band], lon=p) for p in east])
    yield
    end(copies)
    n = outs[0].shape[0]
    for k, dst in enumerate(outs):
        dst[...] = whole[k * n:(k + 1) * n].astype(F32)
    yield


def body(fields, down_weight, mid_weight, up_weight, cotangent):
    _, rows, full, ch = fields.shape
    half, cols = rows // 2, full // 2
    wide = cols + 2 * EDGE
    n_lat, n_lon = lax.axis_size("lat"), lax.axis_size("lon")
    cells = lax.axis_size("dp") * rows * n_lat * full * n_lon
    scale = 1.0 / math.sqrt(cells)
    k = 2 * ch
    vm = pl.BlockSpec(memory_space=pltpu.VMEM)

    def sds(shape, dtype=BF):
        return jax.ShapeDtypeStruct(shape, dtype)

    f, c = fields[0], cotangent[0]
    unit = n_lat * n_lon * 16
    taps = 9 * (ch // 2)

    def sums(count):
        padded = -(-count * taps // unit) * unit
        share, piece = padded // n_lon, padded // (n_lon * n_lat)
        return [
            pltpu.VMEM((2, padded, ch), BF),
            pltpu.VMEM((padded, ch), BF),
            pltpu.VMEM((padded, ch), BF),
            pltpu.VMEM((n_lon - 1, share, ch), BF),
            pltpu.VMEM((share, ch), BF),
            pltpu.VMEM((n_lat - 1, piece, ch), BF),
            pltpu.VMEM((padded, ch), BF),
            pltpu.VMEM((padded, ch), F32),
        ]

    count = 16 + 2 * (1 + 2 * (n_lon - 1) + 2 * (n_lat - 1))
    hbm = pl.BlockSpec(memory_space=pl.ANY)
    out, gout, *terms = pl.pallas_call(
        functools.partial(level, scale),
        out_shape=(sds((rows, full, ch)), sds((rows, full, ch))) + (sds((taps, ch), F32),) * 3,
        in_specs=[hbm] * 5,
        out_specs=(vm,) * 5,
        scratch_shapes=[
            pltpu.VMEM((rows, full, ch), BF),
            pltpu.VMEM((rows, full, ch), BF),
            pltpu.VMEM((2, 2, 8, full, ch), BF),
            pltpu.VMEM((half, 16, ch), BF),
            pltpu.VMEM((half, 16, ch), BF),
            pltpu.VMEM((half // 2, 16, ch), BF),
            pltpu.VMEM((2, 4, 16, ch), BF),
            pltpu.VMEM((2, 4, 16, ch), BF),
            pltpu.VMEM((2, 2, 16, ch), BF),
            pltpu.VMEM((half, 16, ch), BF),
            pltpu.VMEM((half, 16, ch), BF),
            pltpu.VMEM((half // 2, 16, ch), BF),
            pltpu.VMEM((3, 3, 3, ch, ch), BF),
            pltpu.SemaphoreType.DMA((5,)),
            pltpu.SemaphoreType.DMA((count,)),
            pltpu.SemaphoreType.DMA((count,)),
            pltpu.VMEM((half + 9, 2, wide, k), BF),
            pltpu.VMEM((half + 9, 2, wide, k), BF),
            pltpu.VMEM((8, full + 4 * HALO, ch), F32),
            pltpu.VMEM((8, 2, full, ch), F32),
            pltpu.VMEM((3 * k, k), BF),
            pltpu.VMEM((3 * k, k), BF),
            pltpu.VMEM((2 * k, 3 * k), BF),
            pltpu.VMEM((2 * k, 3 * k), BF),
            pltpu.VMEM((3 * k, k), BF),
            pltpu.VMEM((3 * k, k), BF),
            pltpu.VMEM(((half + 8) // 2, wide, k), BF),
            pltpu.VMEM(((half + 4) // 2, 2, wide, 3 * ch), BF),
            pltpu.VMEM(((half + 4) // 2, wide, k), BF),
            pltpu.VMEM(((half + 4) // 2, 2, wide, k), BF),
            pltpu.VMEM(((half + 2) // 2, 2, wide, k), BF),
            pltpu.VMEM((k, 3 * k), F32),
            pltpu.VMEM((3 * ch, 3 * ch), F32),
            pltpu.VMEM((k, 3 * k), F32),
        ] + sums(2) + sums(1),
        compiler_params=pltpu.CompilerParams(
            collective_id=0, has_side_effects=True, vmem_limit_bytes=56 << 20),
    )(f, c, down_weight, mid_weight, up_weight)
    return (out[None], gout[None]) + tuple(t.reshape(3, 3, ch // 2, ch) for t in terms)


def solution(mesh):
    maps = P("dp", "lat", "lon", None)
    kernel = P(None, None, "dp", None)
    return jax.shard_map(
        body,
        mesh=mesh,
        in_specs=(maps, kernel, kernel, kernel, maps),
        out_specs=(maps, maps, kernel, kernel, kernel),
        check_vma=False,
    )
```

time: 236 us -> 64.6 us (0.27)
  blocking collectives: 91 us -> 0 us
  local copies, waits for them, and re-layouts: 58.7 us -> 7.36 us
  Pallas kernels: 23.9 us -> 56.4 us
  waiting for transfers between devices: 27.8 us -> 0 us
  between operations: 14.1 us -> 0.66 us
  other arithmetic: 10.1 us -> 0 us
  starting transfers between devices: 9.27 us -> 0 us
    psum x1 -> x0, blocking collectives: 88.6 us -> none  [body(): total = lax.psum(mine.astype(F32), ('lat', 'lon'))]
    concatenate x2 -> x0, local copies, waits for them, and re-layouts: 33.8 us -> none  [the longest x1 33.7 us: body(): whole = jnp.concatenate([gap, low, tall, high, gap], axis=2)]
    pallas_call x1, Pallas kernels: 23.9 us -> 56.4 us  [body(): pl.pallas_call(functools.partial(level, scale), out_shape=(sds((rows, ful...]
    ppermute x4 -> x0, waiting for transfers between devices: 27.8 us -> none  [the longest x2 17.4 us: shifted(): lax.ppermute(lax.slice_in_dim(x, x.shape[dim] - width, None, axis=dim), a...]
    reshape x3 -> x0, local copies, waits for them, and re-layouts: 16.7 us -> none  [the longest x1 8.61 us: body(): x = jnp.stack([fields[0], cotangent[0]]).reshape(2, rows, cols, 2 * ch)]
    ppermute x4 -> x0, starting transfers between devices: 9.23 us -> none  [the longest x2 6.5 us: shifted(): lax.ppermute(lax.slice_in_dim(x, x.shape[dim] - width, None, axis=dim), a...]
    slice x4 -> x0, local copies, waits for them, and re-layouts: 8.04 us -> none  [the longest x1 5.53 us: body(): whole[1]]
    unnamed x10 -> x13, local copies, waits for them, and re-layouts: 0.02 us -> 7.36 us
  transfers between devices with their start and end apart: 5 -> 0, of which waited for: 4 -> 0; matrix products, arithmetic and copies ran while one was open for 4% -> 0% of each run, Pallas kernels for 0% -> 0%
where the time goes in v2:
time: 64.6 us; the launch traced here: 64.5 us
  Pallas kernels  56.4 us (87%)
  local copies, waits for them, and re-layouts  7.36 us (11%)
  between operations  0.66 us (1%)
    pallas_call x1, Pallas kernels, body(): pl.pallas_call(functools.partial(level, scale), out_shape=(sds((rows, ful...  56.4 us
    unnamed x13, local copies, waits for them, and re-layouts  7.36 us

profile of v2, /device:TPU:0, one launch (start us, length us, event | category | flops | bytes accessed | tf_op | source)
XLA Modules:
  0.0 64.5 jit_solution(14638311100650851446)
XLA Ops:
  0.6 56.4 %shard_map.92 = (bf16[80,128,128]{2,1,0:T(8,128)(2,1)}, bf16[80,128,128]{2,1,0:T(8,128)(2,1)}, f32[576,128]{1,0:T(8,128)}, f32[576,128]{1,0:T(8,128)}, f32[576,128]{1,0:T(8,128)}) custom-call(bf16[80,128,128]{2,1,0:T(8,128)(2,1)} %bitcast.7, bf16[80,128,128]{2,1,0:T(8,128)(2,1)} %bitcast.8, bf16[3,3,64,128]{3,2,1,0:T(8,128)(2,1)} %wd_in.1, ...), custom_call_target="tpu_custom_call" | custom-call | tf_op jit(solution)/shard_map/pallas_call | solution.py:503
  57.1 0.0 copy-start
  57.1 3.7 %copy.15 = bf16[1,80,128,128]{3,2,1,0:T(8,128)(2,1)} copy(bf16[1,80,128,128]{3,2,1,0:T(8,128)(2,1)} %bitcast.10) | data formatting | bytes 5242880
  60.8 0.0 copy-done
  60.8 0.0 copy-start.3
  60.8 0.0 copy-start.2
  60.8 0.0 copy-start.1
  60.8 1.5 %copy.16 = bf16[1,80,128,128]{3,2,1,0:T(8,128)(2,1)} copy(bf16[1,80,128,128]{3,2,1,0:T(8,128)(2,1)S(1)} %bitcast.9) | data formatting | bytes 5242880
  62.3 0.0 copy-done.3
  62.3 0.7 %copy.17 = f32[3,3,64,128]{3,2,1,0:T(8,128)} copy(f32[3,3,64,128]{3,2,1,0:T(8,128)S(1)} %bitcast.13) | data formatting | bytes 589824
  63.0 0.0 copy-done.2
  63.0 0.7 %copy.18 = f32[3,3,64,128]{3,2,1,0:T(8,128)} copy(f32[3,3,64,128]{3,2,1,0:T(8,128)S(1)} %bitcast.12) | data formatting | bytes 589824
  63.7 0.0 copy-done.1
  63.7 0.7 %copy.19 = f32[3,3,64,128]{3,2,1,0:T(8,128)} copy(f32[3,3,64,128]{3,2,1,0:T(8,128)S(1)} %bitcast.11) | data formatting | bytes 589824
Async XLA Ops:
  57.1 3.7 %copy-start = (bf16[80,128,128]{2,1,0:T(8,128)(2,1)S(1)}, bf16[80,128,128]{2,1,0:T(8,128)(2,1)}, u32[]{:S(2)}) copy-start(bf16[80,128,128]{2,1,0:T(8,128)(2,1)} %get-tuple-element.11) | copy-start | bytes 7864324
  60.8 1.5 %copy-start.3 = (f32[576,128]{1,0:T(8,128)S(1)}, f32[576,128]{1,0:T(8,128)}, u32[]{:S(2)}) copy-start(f32[576,128]{1,0:T(8,128)} %get-tuple-element.12) | copy-start | bytes 884740
  60.8 2.2 %copy-start.2 = (f32[576,128]{1,0:T(8,128)S(1)}, f32[576,128]{1,0:T(8,128)}, u32[]{:S(2)}) copy-start(f32[576,128]{1,0:T(8,128)} %get-tuple-element.13) | copy-start | bytes 884740
  60.8 2.9 %copy-start.1 = (f32[576,128]{1,0:T(8,128)S(1)}, f32[576,128]{1,0:T(8,128)}, u32[]{:S(2)}) copy-start(f32[576,128]{1,0:T(8,128)} %get-tuple-element.14) | copy-start | bytes 884740

commit v3 on v2

--- a/solution.py
+++ b/solution.py
@@ -50,7 +50,8 @@
     return x.reshape(x.shape[0] * x.shape[1], x.shape[2])
 
 
-def level(scale, f_in, c_in, wd_in, wm_in, wu_in, out, gout, down_out, mid_out, up_out,
+def level(scale, f_in, c_in, wd_in, wm_in, wu_in, out_hbm, gout_hbm, down_out, mid_out, up_out,
+          out, gout, leave,
           raw_f, raw_c, rows_in, low_in, high_in, pair_in, low_at, high_at, pair_at,
           low_out, high_out, pair_out, w_in, local, send, recv,
           f, c, tmp, otmp, bd, bg, bm, bn, bu, bf, dp, gps, gpp, s1, s2, acc_u, acc_m, acc_d,
@@ -95,9 +96,12 @@
 
     part = ch // 2
     mine = pl.ds(pl.multiple_of(core * part, part), part)
-    loads = [pltpu.make_async_copy(f_in, raw_f, local.at[0]), pltpu.make_async_copy(c_in, raw_c, local.at[1])]
+    loads = []
+    for place in (pl.ds(0, 16), pl.ds(full - 16, 16), pl.ds(16, full - 32)):
+        for src, dst in ((f_in, raw_f), (c_in, raw_c)):
+            loads.append(pltpu.make_async_copy(src.at[:, place], dst.at[:, place], local.at[len(loads)]))
     for i, w in enumerate((wd_in, wm_in, wu_in)):
-        loads.append(pltpu.make_async_copy(w, w_in.at[i, :, :, mine, :], local.at[2 + i]))
+        loads.append(pltpu.make_async_copy(w, w_in.at[i, :, :, mine, :], local.at[len(loads)]))
     for load in loads:
         load.start()
     pl.semaphore_wait(barrier, n_lon + n_lat - 1 + 2 * below.astype(jnp.int32) + 2 * above.astype(jnp.int32))
@@ -128,8 +132,8 @@
     for copy, sends, _ in halos:
         under(sends, copy.start)
 
-    loads[0].wait()
-    loads[1].wait()
+    for load in loads[:4]:
+        load.wait()
 
     def slots(n):
         return lax.broadcasted_iota(jnp.int32, (n, HALO, ch), 1)
@@ -155,7 +159,7 @@
         halos.append((remote(pair_out.at[here], pair_at.at[d], lat=to, lon=east[-1]), sends, gets))
     for copy, sends, _ in halos[early:]:
         under(sends, copy.start)
-    for load in loads[2:]:
+    for load in loads[4:]:
         load.wait()
 
     def landed(part_of):
@@ -410,10 +414,18 @@
     n_up = 8
     steps = half // n_up
     cuts = [steps * i // 5 for i in range(6)]
+    leaving = []
     for i in range(5):
         lax.fori_loop(cuts[i], cuts[i + 1], up_step, 0)
+        band = pl.ds(cuts[i] * 2 * n_up, (cuts[i + 1] - cuts[i]) * 2 * n_up)
+        for src, dst in ((out, out_hbm), (gout, gout_hbm)):
+            copy = pltpu.make_async_copy(src.at[band], dst.at[band], leave.at[len(leaving)])
+            copy.start()
+            leaving.append(copy)
         next(batch_b, None)
         next(batch_a, None)
+    for copy in leaving:
+        copy.wait()
 
 
 def total_of(remote, refs, outs, lat, lon, core, north, east):
@@ -467,6 +479,12 @@
     yield
 
 
+def handed_on(*refs):
+    count = len(refs) // 2
+    for src, dst in zip(refs[:count], refs[count:]):
+        dst[...] = src[...]
+
+
 def body(fields, down_weight, mid_weight, up_weight, cotangent):
     _, rows, full, ch = fields.shape
     half, cols = rows // 2, full // 2
@@ -504,8 +522,11 @@
         functools.partial(level, scale),
         out_shape=(sds((rows, full, ch)), sds((rows, full, ch))) + (sds((taps, ch), F32),) * 3,
         in_specs=[hbm] * 5,
-        out_specs=(vm,) * 5,
+        out_specs=(hbm,) * 2 + (vm,) * 3,
         scratch_shapes=[
+            pltpu.VMEM((rows, full, ch), BF),
+            pltpu.VMEM((rows, full, ch), BF),
+            pltpu.SemaphoreType.DMA((10,)),
             pltpu.VMEM((rows, full, ch), BF),
             pltpu.VMEM((rows, full, ch), BF),
             pltpu.VMEM((2, 2, 8, full, ch), BF),
@@ -519,7 +540,7 @@
             pltpu.VMEM((half, 16, ch), BF),
             pltpu.VMEM((half // 2, 16, ch), BF),
             pltpu.VMEM((3, 3, 3, ch, ch), BF),
-            pltpu.SemaphoreType.DMA((5,)),
+            pltpu.SemaphoreType.DMA((9,)),
             pltpu.SemaphoreType.DMA((count,)),
             pltpu.SemaphoreType.DMA((count,)),
             pltpu.VMEM((half + 9, 2, wide, k), BF),
@@ -544,6 +565,21 @@
         compiler_params=pltpu.CompilerParams(
             collective_id=0, has_side_effects=True, vmem_limit_bytes=56 << 20),
     )(f, c, down_weight, mid_weight, up_weight)
+    results = (out, gout, *terms)
+
+    def blocked(x):
+        shape = (x.shape[0] // 4,) + x.shape[1:]
+        return pl.BlockSpec(shape, lambda i: (i,) + (0,) * (len(shape) - 1))
+
+    specs = tuple(blocked(x) for x in results)
+    out, gout, *terms = pl.pallas_call(
+        handed_on,
+        grid=(4,),
+        out_shape=tuple(sds(x.shape, x.dtype) for x in results),
+        in_specs=list(specs),
+        out_specs=specs,
+        compiler_params=pltpu.CompilerParams(vmem_limit_bytes=56 << 20),
+    )(*results)
     return (out[None], gout[None]) + tuple(t.reshape(3, 3, ch // 2, ch) for t in terms)
 
 

time: 64.6 us -> 61.2 us (0.947)
  local copies, waits for them, and re-layouts: 7.36 us -> 0 us
  Pallas kernels: 56.4 us -> 60.3 us
    unnamed x13 -> x0, local copies, waits for them, and re-layouts: 7.36 us -> none
    pallas_call x0 -> x1, Pallas kernels: none -> 5.7 us  [body(): pl.pallas_call(handed_on, grid=(4,), out_shape=tuple((sds(x.shape, x.dtyp...]
    pallas_call x1, Pallas kernels: 56.4 us -> 54.6 us  [body(): pl.pallas_call(functools.partial(level, scale), out_shape=(sds((rows, ful...]
where the time goes in v3:
time: 61.2 us; the launch traced here: 61 us
  Pallas kernels  60.3 us (99%)
  between operations  0.64 us (1%)
    pallas_call x1, Pallas kernels, body(): pl.pallas_call(functools.partial(level, scale), out_shape=(sds((rows, ful...  54.6 us
    pallas_call x1, Pallas kernels, body(): pl.pallas_call(handed_on, grid=(4,), out_shape=tuple((sds(x.shape, x.dtyp...  5.7 us

profile of v3, /device:TPU:0, one launch (start us, length us, event | category | flops | bytes accessed | tf_op | source)
XLA Modules:
  0.0 61.0 jit_solution(8453229755084516360)
XLA Ops:
  0.6 54.6 %shard_map.92 = (bf16[80,128,128]{2,1,0:T(8,128)(2,1)}, bf16[80,128,128]{2,1,0:T(8,128)(2,1)}, f32[576,128]{1,0:T(8,128)}, f32[576,128]{1,0:T(8,128)}, f32[576,128]{1,0:T(8,128)}) custom-call(bf16[80,128,128]{2,1,0:T(8,128)(2,1)} %bitcast.7, bf16[80,128,128]{2,1,0:T(8,128)(2,1)} %bitcast.8, bf16[3,3,64,128]{3,2,1,0:T(8,128)(2,1)} %wd_in.1, ...), custom_call_target="tpu_custom_call" | custom-call | tf_op jit(solution)/shard_map/pallas_call | solution.py:521
  55.3 5.7 %shard_map.93 = (bf16[80,128,128]{2,1,0:T(8,128)(2,1)}, bf16[80,128,128]{2,1,0:T(8,128)(2,1)}, f32[576,128]{1,0:T(8,128)}, f32[576,128]{1,0:T(8,128)}, f32[576,128]{1,0:T(8,128)}) custom-call(bf16[80,128,128]{2,1,0:T(8,128)(2,1)} %get-tuple-element.15.refs_0_, bf16[80,128,128]{2,1,0:T(8,128)(2,1)} %get-tuple-element.16.refs_1_, ...), custom_call_target="tpu_custom_call" | custom-call | tf_op jit(solution)/shard_map/pallas_call | solution.py:575

commit v4 on v3

--- a/solution.py
+++ b/solution.py
@@ -568,13 +568,13 @@
     results = (out, gout, *terms)
 
     def blocked(x):
-        shape = (x.shape[0] // 4,) + x.shape[1:]
+        shape = (x.shape[0] // 8,) + x.shape[1:]
         return pl.BlockSpec(shape, lambda i: (i,) + (0,) * (len(shape) - 1))
 
     specs = tuple(blocked(x) for x in results)
     out, gout, *terms = pl.pallas_call(
         handed_on,
-        grid=(4,),
+        grid=(8,),
         out_shape=tuple(sds(x.shape, x.dtype) for x in results),
         in_specs=list(specs),
         out_specs=specs,

time: 61.2 us -> 63.1 us (1.031)
  Pallas kernels: 60.3 us -> 62.2 us
    pallas_call x1, Pallas kernels: 5.7 us -> 7.58 us  [body(): pl.pallas_call(handed_on, grid=(8,), out_shape=tuple((sds(x.shape, x.dtyp...]
where the time goes in v4:
time: 63.1 us; the launch traced here: 62.8 us
  Pallas kernels  62.2 us (99%)
  between operations  0.64 us (1%)
    pallas_call x1, Pallas kernels, body(): pl.pallas_call(functools.partial(level, scale), out_shape=(sds((rows, ful...  54.6 us
    pallas_call x1, Pallas kernels, body(): pl.pallas_call(handed_on, grid=(8,), out_shape=tuple((sds(x.shape, x.dtyp...  7.58 us

profile of v4, /device:TPU:0, one launch (start us, length us, event | category | flops | bytes accessed | tf_op | source)
XLA Modules:
  0.0 62.8 jit_solution(8057522744878864385)
XLA Ops:
  0.6 54.6 %shard_map.92 = (bf16[80,128,128]{2,1,0:T(8,128)(2,1)}, bf16[80,128,128]{2,1,0:T(8,128)(2,1)}, f32[576,128]{1,0:T(8,128)}, f32[576,128]{1,0:T(8,128)}, f32[576,128]{1,0:T(8,128)}) custom-call(bf16[80,128,128]{2,1,0:T(8,128)(2,1)} %bitcast.7, bf16[80,128,128]{2,1,0:T(8,128)(2,1)} %bitcast.8, bf16[3,3,64,128]{3,2,1,0:T(8,128)(2,1)} %wd_in.1, ...), custom_call_target="tpu_custom_call" | custom-call | tf_op jit(solution)/shard_map/pallas_call | solution.py:521
  55.3 7.6 %shard_map.93 = (bf16[80,128,128]{2,1,0:T(8,128)(2,1)}, bf16[80,128,128]{2,1,0:T(8,128)(2,1)}, f32[576,128]{1,0:T(8,128)}, f32[576,128]{1,0:T(8,128)}, f32[576,128]{1,0:T(8,128)}) custom-call(bf16[80,128,128]{2,1,0:T(8,128)(2,1)} %get-tuple-element.15.refs_0_, bf16[80,128,128]{2,1,0:T(8,128)(2,1)} %get-tuple-element.16.refs_1_, ...), custom_call_target="tpu_custom_call" | custom-call | tf_op jit(solution)/shard_map/pallas_call | solution.py:575
